TPU v7x, 32 devices: a whole 2x2x4 slice. The times are simulated.
32 devices in a mesh: dp: 8 (over y, x, core), chan: 4 (over z).
Axes of the slice: x: 2, y: 2, z: 4, core: 2. Of those that a mesh axis runs over, the one named last changes fastest.
Arguments:
- mel_input: bfloat16 [80, 32, 1536], P('chan', 'dp'), may hold values from -6 to 6
- w_conv1: bfloat16 [3, 80, 768], replicated, may hold values from -0.375 to 0.375
- b_conv1: bfloat16 [768], replicated, may hold values from -4 to 4
- w_conv2: bfloat16 [3, 768, 768], replicated, may hold values from -0.125 to 0.125
- b_conv2: bfloat16 [768], replicated, may hold values from -4 to 4
- gain_attn: bfloat16 [768], replicated, may hold values from 0.5 to 1.5
- bias_attn: bfloat16 [768], replicated, may hold values from -3 to 3
- w_qkv: bfloat16 [768, 2304], replicated, may hold values from -0.375 to 0.375
- b_query: bfloat16 [768], replicated, may hold values from -4 to 4
- b_value: bfloat16 [768], replicated, may hold values from -0.75 to 0.75
- w_out: bfloat16 [768, 768], replicated, may hold values from -0.21875 to 0.21875
- b_out: bfloat16 [768], replicated, may hold values from -4 to 4
- gain_mlp: bfloat16 [768], replicated, may hold values from 0.5 to 1.5
- bias_mlp: bfloat16 [768], replicated, may hold values from -3 to 3
- w_up: bfloat16 [768, 3072], replicated, may hold values from -0.21875 to 0.21875
- b_up: bfloat16 [3072], replicated, may hold values from -4 to 4
- w_down: bfloat16 [3072, 768], replicated, may hold values from -0.109375 to 0.109375
- b_down: bfloat16 [768], replicated, may hold values from -4 to 4
- target: bfloat16 [32, 768, 768], P(('dp', 'chan')), may hold values from -12 to 12
- lengths: int32 [32], replicated, may hold values from 256 to 768, as said below
- row_clip: int32 [32], replicated, may hold values from 0 to 31, each once
- language: int32 [32], replicated, may hold values from 0 to 98
Outputs:
- block_out: bfloat16 [32, 768, 768], P(('dp', 'chan'))
- group_loss: float32 [99], replicated
- grad_mel: bfloat16 [80, 32, 1536], P('chan', 'dp')
- grad_w_conv1: float32 [3, 80, 768], P(None, 'chan', 'dp')
- grad_b_conv1: float32 [768], replicated
- grad_w_conv2: float32 [3, 768, 768], P(None, 'chan', 'dp')
- grad_b_conv2: float32 [768], replicated
- grad_gain_attn: float32 [768], replicated
- grad_bias_attn: float32 [768], replicated
- grad_w_qkv: float32 [768, 2304], P('dp', 'chan')
- grad_b_query: float32 [768], replicated
- grad_b_value: float32 [768], replicated
- grad_w_out: float32 [768, 768], P('dp', 'chan')
- grad_b_out: float32 [768], replicated
- grad_gain_mlp: float32 [768], replicated
- grad_bias_mlp: float32 [768], replicated
- grad_w_up: float32 [768, 3072], P('dp', 'chan')
- grad_b_up: float32 [3072], replicated
- grad_w_down: float32 [3072, 768], P('dp', 'chan')
- grad_b_down: float32 [768], replicated
Inputs may be any that keep to these rules, and one draw needn't show every extreme that they name: `lengths`: valid downsampled frames of each clip; some clip has all 768. `row_clip`: each clip number appears once.
All inputs are finite; a program needn't handle non-finite values.
Results may differ from a plain program's by a relative error of at most 0.017.
Values may be sent and summed in bfloat16 or wider, within the bound.
A program may use at most 256 MiB of HBM per device.

v0:
```python
import math

import jax
import jax.numpy as jnp
from jax import lax
from jax.sharding import PartitionSpec as P

HEAD_DIM = 64
GROUPS = 99


epsilon = 1e-05
masked_score = -1e30


def gelu_exact(values):
    return jax.nn.gelu(values, approximate=False)


def normalize(values, ln_gain, ln_bias):
    average = jnp.mean(values, axis=-1, keepdims=True)
    centred = values - average
    variance = jnp.mean(centred * centred, axis=-1, keepdims=True)
    return centred * lax.rsqrt(variance + epsilon) * ln_gain + ln_bias


def sinusoids(length, channels):
    half_width = channels // 2
    increment = math.log(10000.0) / (half_width - 1)
    inverse = jnp.exp(-increment * jnp.arange(half_width, dtype=jnp.float32))
    angles = jnp.arange(length, dtype=jnp.float32)[:, None] * inverse[None, :]
    return jnp.concatenate([jnp.sin(angles), jnp.cos(angles)], axis=1)


def lookup(row_ids, table):
    matches = row_ids[:, None] == jnp.arange(table.shape[0], dtype=jnp.int32)[None, :]
    return jnp.sum(jnp.where(matches, table[None, :], 0), axis=1)


def taps_stride_one(signal):
    padded = jnp.pad(signal, ((0, 0), (0, 0), (1, 1)))
    length = signal.shape[2]
    return [
        padded[:, :, offset : offset + length].reshape(signal.shape[0], -1) for offset in range(3)
    ]


def taps_stride_two(signal):
    padded = jnp.pad(signal, ((0, 0), (0, 0), (1, 1)))
    length = signal.shape[2] // 2
    return [
        padded[:, :, offset : offset + 2 * length : 2].reshape(signal.shape[0], -1)
        for offset in range(3)
    ]


def conv_channel_major(weight, taps):
    total = lax.dot_general(
        weight[0], taps[0], (((0,), (0,)), ((), ())), preferred_element_type=jnp.float32
    )
    for offset in (1, 2):
        total = total + lax.dot_general(
            weight[offset],
            taps[offset],
            (((0,), (0,)), ((), ())),
            preferred_element_type=jnp.float32,
        )
    return total


def conv_frame_major(taps, weight):
    total = lax.dot_general(
        taps[0], weight[0], (((0,), (0,)), ((), ())), preferred_element_type=jnp.float32
    )
    for offset in (1, 2):
        total = total + lax.dot_general(
            taps[offset],
            weight[offset],
            (((0,), (0,)), ((), ())),
            preferred_element_type=jnp.float32,
        )
    return total


def stride_one_back(parts):
    edge = jnp.zeros_like(parts[0][:, :, :1])
    ahead = jnp.concatenate([parts[0][:, :, 1:], edge], axis=2)
    behind = jnp.concatenate([edge, parts[2][:, :, :-1]], axis=2)
    return ahead + parts[1] + behind


def stride_two_back(parts):
    edge = jnp.zeros_like(parts[0][:, :, :1])
    odd_terms = parts[2] + jnp.concatenate([parts[0][:, :, 1:], edge], axis=2)
    fill = jnp.zeros((), parts[1].dtype)
    even_spread = lax.pad(parts[1], fill, ((0, 0, 0), (0, 0, 0), (0, 1, 1)))
    odd_spread = lax.pad(odd_terms, fill, ((0, 0, 0), (0, 0, 0), (1, 0, 1)))
    return even_spread + odd_spread


def back_channel_major(weight, taps, grads, clip_count, length):
    weight_grad = jnp.stack(
        [
            lax.dot_general(
                taps[offset], grads, (((1,), (1,)), ((), ())), preferred_element_type=jnp.float32
            )
            for offset in range(3)
        ]
    )
    parts = [
        lax.dot_general(
            weight[offset], grads, (((1,), (0,)), ((), ())), preferred_element_type=jnp.float32
        ).reshape(weight.shape[1], clip_count, length)
        for offset in range(3)
    ]
    return (weight_grad, stride_one_back(parts))


def back_frame_major(weight, taps, grads, clip_count, length):
    weight_grad = jnp.stack(
        [
            lax.dot_general(
                taps[offset], grads, (((1,), (0,)), ((), ())), preferred_element_type=jnp.float32
            )
            for offset in range(3)
        ]
    )
    parts = [
        lax.dot_general(
            weight[offset], grads, (((1,), (1,)), ((), ())), preferred_element_type=jnp.float32
        ).reshape(weight.shape[1], clip_count, length)
        for offset in range(3)
    ]
    return (weight_grad, stride_two_back(parts))


def to_pairs(block, clip_count, length):
    pair_count = block.shape[1] // (2 * HEAD_DIM)
    return (
        block.reshape(clip_count, length, pair_count, 2 * HEAD_DIM)
        .transpose(0, 2, 1, 3)
        .reshape(clip_count * pair_count, length, 2 * HEAD_DIM)
    )


def from_pairs(items, clip_count, length):
    pair_count = items.shape[0] // clip_count
    return (
        items.reshape(clip_count, pair_count, length, 2 * HEAD_DIM)
        .transpose(0, 2, 1, 3)
        .reshape(clip_count * length, pair_count * 2 * HEAD_DIM)
    )


def pair_scores(query_heads, key_heads, key_ok):
    scores = jnp.einsum(
        "qhd,khd->hqk", query_heads, key_heads, preferred_element_type=jnp.float32
    ) * HEAD_DIM ** (-0.5)
    return jnp.where(key_ok[None, None, :], scores, masked_score)


def attend_item(pieces):
    query_pair, key_pair, value_pair, key_ok = pieces
    length = query_pair.shape[0]
    query_heads = query_pair.reshape(length, 2, HEAD_DIM)
    key_heads = key_pair.reshape(length, 2, HEAD_DIM)
    value_heads = value_pair.reshape(length, 2, HEAD_DIM)
    scores = pair_scores(query_heads, key_heads, key_ok)
    row_max = jnp.max(scores, axis=-1, keepdims=True)
    exponent = jnp.exp(scores - row_max)
    totals = jnp.sum(exponent, axis=-1, keepdims=True)
    attention = exponent / totals
    context = jnp.einsum(
        "hqk,khd->qhd",
        attention.astype(jnp.bfloat16),
        value_heads,
        preferred_element_type=jnp.float32,
    )
    return (
        context.reshape(length, 2 * HEAD_DIM).astype(jnp.bfloat16),
        (row_max + jnp.log(totals))[..., 0],
    )


def attend_back(pieces):
    query_pair, key_pair, value_pair, key_ok, log_total, grad_pair = pieces
    length = query_pair.shape[0]
    query_heads = query_pair.reshape(length, 2, HEAD_DIM)
    key_heads = key_pair.reshape(length, 2, HEAD_DIM)
    value_heads = value_pair.reshape(length, 2, HEAD_DIM)
    grad_heads = grad_pair.reshape(length, 2, HEAD_DIM)
    scores = pair_scores(query_heads, key_heads, key_ok)
    attention = jnp.exp(scores - log_total[..., None])
    grad_attention = jnp.einsum(
        "qhd,khd->hqk", grad_heads, value_heads, preferred_element_type=jnp.float32
    )
    row_inner = jnp.sum(attention * grad_attention, axis=-1, keepdims=True)
    grad_scores = (attention * (grad_attention - row_inner)).astype(jnp.bfloat16)
    score_scale = HEAD_DIM ** (-0.5)
    grad_query = (
        (
            jnp.einsum("hqk,khd->qhd", grad_scores, key_heads, preferred_element_type=jnp.float32)
            * score_scale
        )
        .reshape(length, -1)
        .astype(jnp.bfloat16)
    )
    grad_key = (
        (
            jnp.einsum("hqk,qhd->khd", grad_scores, query_heads, preferred_element_type=jnp.float32)
            * score_scale
        )
        .reshape(length, -1)
        .astype(jnp.bfloat16)
    )
    grad_value = (
        jnp.einsum(
            "hqk,qhd->khd",
            attention.astype(jnp.bfloat16),
            grad_heads,
            preferred_element_type=jnp.float32,
        )
        .reshape(length, -1)
        .astype(jnp.bfloat16)
    )
    return (grad_query, grad_key, grad_value)


def column_sum(values):
    return jnp.sum(values.astype(jnp.float32), axis=0)


def on_device(
    mel_input,
    w_conv1,
    b_conv1,
    w_conv2,
    b_conv2,
    gain_attn,
    bias_attn,
    w_qkv,
    b_query,
    b_value,
    w_out,
    b_out,
    gain_mlp,
    bias_mlp,
    w_up,
    b_up,
    w_down,
    b_down,
    target,
    lengths,
    row_clip,
    language,
):
    clip_count, frame_count, model_width = target.shape
    mel_count = mel_input.shape[2]
    chan_count = lax.axis_size("chan")
    chan_at = lax.axis_index("chan")
    data_at = lax.axis_index("dp")
    group_count = clip_count * chan_count
    own_ids = lax.dynamic_slice_in_dim(
        row_clip, data_at * group_count + chan_at * clip_count, clip_count
    )
    valid_len = lookup(own_ids, lengths)
    frame_ok = jnp.arange(frame_count, dtype=jnp.int32)[None, :] < valid_len[:, None]
    positions = sinusoids(frame_count, model_width)
    slab = model_width // chan_count
    slab_start = chan_at * slab
    flat_zero = jnp.zeros((model_width,), jnp.float32)
    bins_local = mel_input.shape[0]
    conv_one_w = lax.dynamic_slice_in_dim(w_conv1, chan_at * bins_local, bins_local, 1)
    conv_two_w = lax.dynamic_slice_in_dim(w_conv2, slab_start, slab, 1)
    taps_one = taps_stride_one(mel_input)
    conv_one = lax.psum_scatter(
        conv_channel_major(conv_one_w, taps_one), "chan", scatter_dimension=0, tiled=True
    )
    conv_one = (
        conv_one + lax.dynamic_slice_in_dim(b_conv1.astype(jnp.float32), slab_start, slab)[:, None]
    )
    act_one, gelu_one_pull = jax.vjp(gelu_exact, conv_one)
    act_one = act_one.astype(jnp.bfloat16).reshape(slab, group_count, mel_count)
    taps_two = taps_stride_two(act_one)
    partial_two = conv_frame_major(taps_two, conv_two_w)
    conv_two = lax.psum_scatter(partial_two, "chan", scatter_dimension=1, tiled=True)
    conv_two = (
        conv_two + lax.dynamic_slice_in_dim(b_conv2.astype(jnp.float32), slab_start, slab)[None, :]
    )
    act_two, gelu_two_pull = jax.vjp(gelu_exact, conv_two)
    pos_local = lax.dynamic_slice_in_dim(positions, slab_start, slab, 1)
    stem_local = (act_two.reshape(group_count, frame_count, slab) + pos_local[None]).astype(
        jnp.bfloat16
    )
    stem_rows = lax.all_to_all(
        stem_local.reshape(group_count * frame_count, slab),
        "chan",
        split_axis=0,
        concat_axis=1,
        tiled=True,
    )
    stem_float = stem_rows.astype(jnp.float32)
    normed_a, norm_a_pull = jax.vjp(
        normalize, stem_float, gain_attn.astype(jnp.float32), bias_attn.astype(jnp.float32)
    )
    normed_a = normed_a.astype(jnp.bfloat16)
    qkv_bias = jnp.concatenate(
        [b_query.astype(jnp.float32), flat_zero, b_value.astype(jnp.float32)]
    )
    joined = (jnp.dot(normed_a, w_qkv, preferred_element_type=jnp.float32) + qkv_bias).astype(
        jnp.bfloat16
    )
    query_items = to_pairs(joined[:, :model_width], clip_count, frame_count)
    key_items = to_pairs(joined[:, model_width : 2 * model_width], clip_count, frame_count)
    value_items = to_pairs(joined[:, 2 * model_width :], clip_count, frame_count)
    pair_count = model_width // (2 * HEAD_DIM)
    mask_items = jnp.repeat(frame_ok, pair_count, axis=0)
    context_items, log_totals = lax.map(
        attend_item, (query_items, key_items, value_items, mask_items)
    )
    context = from_pairs(context_items, clip_count, frame_count)
    middle = (
        stem_float
        + jnp.dot(context, w_out, preferred_element_type=jnp.float32)
        + b_out.astype(jnp.float32)
    )
    normed_b, norm_b_pull = jax.vjp(
        normalize, middle, gain_mlp.astype(jnp.float32), bias_mlp.astype(jnp.float32)
    )
    normed_b = normed_b.astype(jnp.bfloat16)
    upward = jnp.dot(normed_b, w_up, preferred_element_type=jnp.float32) + b_up.astype(jnp.float32)
    hidden, gelu_up_pull = jax.vjp(gelu_exact, upward)
    hidden = hidden.astype(jnp.bfloat16)
    final_rows = (
        middle
        + jnp.dot(hidden, w_down, preferred_element_type=jnp.float32)
        + b_down.astype(jnp.float32)
    )
    row_ok = frame_ok.reshape(-1, 1).astype(jnp.float32)
    mismatch = (final_rows - target.reshape(-1, model_width).astype(jnp.float32)) * row_ok
    clip_loss = 0.5 * jnp.sum((mismatch * mismatch).reshape(clip_count, -1), axis=1)
    group_ids = jnp.arange(GROUPS, dtype=jnp.int32)
    own_lang = lookup(own_ids, language)
    member_own = (own_lang[:, None] == group_ids[None, :]).astype(jnp.float32)
    group_part = jnp.sum(clip_loss[:, None] * member_own, axis=0)
    contract_rows = (((0,), (0,)), ((), ()))
    contract_cols = (((1,), (1,)), ((), ()))
    grad_branch = mismatch.astype(jnp.bfloat16)
    grad_b_down = column_sum(grad_branch)
    grad_w_down = lax.dot_general(
        hidden, grad_branch, contract_rows, preferred_element_type=jnp.float32
    )
    grad_hidden = lax.dot_general(
        grad_branch, w_down, contract_cols, preferred_element_type=jnp.float32
    )
    grad_up = gelu_up_pull(grad_hidden)[0].astype(jnp.bfloat16)
    grad_b_up = column_sum(grad_up)
    grad_w_up = lax.dot_general(
        normed_b, grad_up, contract_rows, preferred_element_type=jnp.float32
    )
    grad_normed_b = lax.dot_general(
        grad_up, w_up, contract_cols, preferred_element_type=jnp.float32
    )
    grad_mid_norm, grad_gain_mlp, grad_bias_mlp = norm_b_pull(grad_normed_b)
    grad_middle = mismatch + grad_mid_norm
    grad_attended = grad_middle.astype(jnp.bfloat16)
    grad_b_out = column_sum(grad_attended)
    grad_w_out = lax.dot_general(
        context, grad_attended, contract_rows, preferred_element_type=jnp.float32
    )
    grad_context = lax.dot_general(
        grad_attended, w_out, contract_cols, preferred_element_type=jnp.float32
    ).astype(jnp.bfloat16)
    grad_items = to_pairs(grad_context, clip_count, frame_count)
    grad_query_items, grad_key_items, grad_value_items = lax.map(
        attend_back, (query_items, key_items, value_items, mask_items, log_totals, grad_items)
    )
    grad_joined = jnp.concatenate(
        [
            from_pairs(grad_query_items, clip_count, frame_count),
            from_pairs(grad_key_items, clip_count, frame_count),
            from_pairs(grad_value_items, clip_count, frame_count),
        ],
        axis=1,
    )
    grad_b_query = column_sum(grad_joined[:, :model_width])
    grad_b_value = column_sum(grad_joined[:, 2 * model_width :])
    grad_w_qkv = lax.dot_general(
        normed_a, grad_joined, contract_rows, preferred_element_type=jnp.float32
    )
    grad_normed_a = lax.dot_general(
        grad_joined, w_qkv, contract_cols, preferred_element_type=jnp.float32
    )
    grad_stem_norm, grad_gain_attn, grad_bias_attn = norm_a_pull(grad_normed_a)
    grad_stem = (grad_middle + grad_stem_norm).astype(jnp.bfloat16)
    grad_stem_local = lax.all_to_all(grad_stem, "chan", split_axis=1, concat_axis=0, tiled=True)
    grad_two_local = gelu_two_pull(grad_stem_local.astype(jnp.float32))[0].astype(jnp.bfloat16)
    grad_bias_two = lax.dynamic_update_slice(flat_zero, column_sum(grad_two_local), (slab_start,))
    grad_two = lax.all_gather(grad_two_local, "chan", axis=1, tiled=True)
    grad_w_two, grad_act_one = back_frame_major(
        conv_two_w, taps_two, grad_two, group_count, frame_count
    )
    grad_one_local = gelu_one_pull(grad_act_one.reshape(slab, -1))[0].astype(jnp.bfloat16)
    grad_bias_one = lax.dynamic_update_slice(
        flat_zero, jnp.sum(grad_one_local.astype(jnp.float32), axis=1), (slab_start,)
    )
    grad_one = lax.all_gather(grad_one_local, "chan", axis=0, tiled=True)
    grad_w_one, grad_mel_rows = back_channel_major(
        conv_one_w, taps_one, grad_one, group_count, mel_count
    )
    grad_mel = grad_mel_rows.astype(jnp.bfloat16)
    wide_qkv, wide_out, wide_up, wide_down, part_one, part_two = (
        lax.psum_scatter(grad_w_qkv, "dp", scatter_dimension=0, tiled=True),
        lax.psum_scatter(grad_w_out, "dp", scatter_dimension=0, tiled=True),
        lax.psum_scatter(grad_w_up, "dp", scatter_dimension=0, tiled=True),
        lax.psum_scatter(grad_w_down, "dp", scatter_dimension=0, tiled=True),
        lax.psum_scatter(grad_w_one, "dp", scatter_dimension=2, tiled=True),
        lax.psum_scatter(grad_w_two, "dp", scatter_dimension=2, tiled=True),
    )
    final_qkv, final_out, final_up, final_down = (
        lax.psum_scatter(
            wide_qkv.astype(jnp.bfloat16), "chan", scatter_dimension=1, tiled=True
        ).astype(jnp.float32),
        lax.psum_scatter(
            wide_out.astype(jnp.bfloat16), "chan", scatter_dimension=1, tiled=True
        ).astype(jnp.float32),
        lax.psum_scatter(
            wide_up.astype(jnp.bfloat16), "chan", scatter_dimension=1, tiled=True
        ).astype(jnp.float32),
        lax.psum_scatter(
            wide_down.astype(jnp.bfloat16), "chan", scatter_dimension=1, tiled=True
        ).astype(jnp.float32),
    )
    totals_all = lax.psum(
        (
            group_part,
            grad_bias_one,
            grad_bias_two,
            grad_gain_attn,
            grad_bias_attn,
            grad_b_query,
            grad_b_value,
            grad_b_out,
            grad_gain_mlp,
            grad_bias_mlp,
            grad_b_up,
            grad_b_down,
        ),
        ("dp", "chan"),
    )
    member_all = language[:, None] == group_ids[None, :]
    frames_group = jnp.sum(jnp.where(member_all, lengths[:, None], 0), axis=0)
    group_loss = totals_all[0] / (model_width * jnp.maximum(frames_group, 1).astype(jnp.float32))
    block_out = final_rows.astype(jnp.bfloat16).reshape(clip_count, frame_count, model_width)
    return (
        block_out,
        group_loss,
        grad_mel,
        part_one,
        totals_all[1],
        part_two,
        totals_all[2],
        totals_all[3],
        totals_all[4],
        final_qkv,
        totals_all[5],
        totals_all[6],
        final_out,
        totals_all[7],
        totals_all[8],
        totals_all[9],
        final_up,
        totals_all[10],
        final_down,
        totals_all[11],
    )


def solution(mesh):
    placed = (
        P("chan", "dp", None),
        P(),
        P(),
        P(),
        P(),
        P(),
        P(),
        P(),
        P(),
        P(),
        P(),
        P(),
        P(),
        P(),
        P(),
        P(),
        P(),
        P(),
        P(("dp", "chan"), None, None),
        P(),
        P(),
        P(),
    )
    return jax.shard_map(
        on_device,
        mesh=mesh,
        in_specs=placed,
        out_specs=(
            P(("dp", "chan"), None, None),
            P(),
            P("chan", "dp", None),
            P(None, "chan", "dp"),
            P(),
            P(None, "chan", "dp"),
            P(),
            P(),
            P(),
            P("dp", "chan"),
            P(),
            P(),
            P("dp", "chan"),
            P(),
            P(),
            P(),
            P("dp", "chan"),
            P(),
            P("dp", "chan"),
            P(),
        ),
        check_vma=False,
    )
```

profile of v0, /device:TPU:0, one launch (start us, length us, event | category | flops | bytes accessed | tf_op | source)
XLA Modules:
  0.0 1827.5 jit_solution(4631804294564976824)
XLA Ops:
  32.6 20.9 %add_add_fusion = f32[768,6144]{1,0:T(8,128)} fusion(f32[768,6144]{1,0:T(8,128)} %fusion.84, f32[768,6144]{1,0:T(8,128)} %fusion.82, bf16[20,6144]{1,0:T(8,128)(2,1)} %bitcast.348, bf16[3,80,768]{2,1,0:T(8,128)(2,1)} %param.27, s32[]{:T(128)S(6)} %add.271, s32[]{:T(128)S(6)} %select_n.34), kind=kOutput, calls=%fused_computation.37 | convolution fusion | flops 198180864 | bytes 56954888 | tf_op jit(solution)/shard_map/dot_general | solution.py:62
  54.3 315.9 %reduce-scatter.23.cloned.1.call-done = f32[192,6144]{1,0:T(8,128)} async-done(((f32[768,6144]{1,0:T(8,128)}), f32[192,6144]{1,0:T(8,128)}) %reduce-scatter.23.cloned.1.call-update) | async-done | bytes 4718608 | tf_op jit(solution)/shard_map/reduce_scatter | solution.py:276
  370.1 12.8 multiply_convert_fusion.2
  392.7 84.0 %slice.63 = bf16[192,4,768]{2,1,0:T(4,128)(2,1)} slice(bf16[192,4,1538]{2,1,0:T(4,128)(2,1)} %pad.18), slice={[0:192:1], [0:4:1], [0:1536:2]} | slice | bytes 2359296 | tf_op jit(solution)/shard_map/slice | solution.py:52
  476.7 84.0 %slice.65 = bf16[192,4,768]{2,1,0:T(4,128)(2,1)} slice(bf16[192,4,1538]{2,1,0:T(4,128)(2,1)} %pad.18), slice={[0:192:1], [0:4:1], [1:1537:2]} | slice | bytes 2359296 | tf_op jit(solution)/shard_map/slice | solution.py:52
  560.7 84.2 %slice.67 = bf16[192,4,768]{2,1,0:T(4,128)(2,1)} slice(bf16[192,4,1538]{2,1,0:T(4,128)(2,1)} %pad.18), slice={[0:192:1], [0:4:1], [2:1538:2]} | slice | bytes 2359296 | tf_op jit(solution)/shard_map/slice | solution.py:52
  662.6 155.9 %reduce-scatter.25.cloned.1.call-done = f32[3072,192]{0,1:T(8,128)} async-done(((f32[3072,768]{0,1:T(8,128)}), f32[3072,192]{0,1:T(8,128)}) %reduce-scatter.25.cloned.1.call-update) | async-done | bytes 2359312 | tf_op jit(solution)/shard_map/reduce_scatter | solution.py:286
  846.4 15.1 all-to-all-done
  881.3 40.2 %while.26 = (s32[]{:T(128)}, bf16[6,768,128]{1,2,0:T(8,128)(2,1)}, f32[6,2,768]{2,1,0:T(2,128)}, bf16[6,768,128]{1,2,0:T(8,128)(2,1)}, pred[6,768]{1,0:T(8,128)(...) while((s32[]{:T(128)}, bf16[6,768,128]{1,2,0:T(8,128)(2,1)}, ...), condition=%wide.region_8.9_spmd, body=%wide.region_5.8_spmd.sunk | while | flops 316242432 | bytes 16568177 | solution.py:318
  926.7 28.2 %multiply_convert_fusion.1 = (bf16[768,3072]{1,0:T(8,128)(2,1)}, f32[768,3072]{1,0:T(8,128)}, f32[768,3072]{1,0:T(8,128)}) fusion(f32[3072]{0:T(1024)S(1)} %copy-done.40, bf16[768,3072]{1,0:T(8,128)(2,1)S(1)} %bitcast.375, f32[768,768]{0,1:T(8,128)S(1)} %get-tuple-element.284, f32[768]{0:T(1024)S(1)} %copy-done.46, f32[768]{0:T(1024)S(1)} %convert_element_type.259, ...), kind=kOutput, calls=%fused_computation.46 | convolution fusion | flops 3782541312 | bytes 30695424 | tf_op jit(solution)/shard_map/dot_general | solution.py:331
  963.6 13.7 convert_reduce_fusion
  996.5 76.5 %while.27 = (s32[]{:T(128)}, bf16[6,768,128]{1,2,0:T(8,128)(2,1)}, bf16[6,768,128]{1,2,0:T(8,128)(2,1)}, bf16[6,768,128]{1,2,0:T(8,128)(2,1)}, bf16[6,768,128]{1...) while((s32[]{:T(128)}, bf16[6,768,128]{1,2,0:T(8,128)(2,1)}, ...), condition=%wide.region_19.20_spmd, body=%wide.region_17.19_spmd.sunk | while | flops 773159424 | bytes 40155028 | solution.py:375
  1089.8 31.3 %all_to_all.26 = bf16[768,4,192]{0,2,1:T(8,128)(2,1)S(1)} all-to-all(bf16[768,4,192]{0,2,1:T(8,128)(2,1)S(1)} %bitcast.345), channel_id=1, replica_groups=mesh['dp'=8,'chan'=4] {'chan'}, dimensions={1} | all-to-all | bytes 2359296 | tf_op jit(solution)/shard_map/all_to_all | solution.py:396
  1135.0 10.8 fusion.111
  1146.6 10.6 fusion.117
  1160.7 54.5 %all-gather.3.cloned.1.call-done = bf16[3072,768]{0,1:T(8,128)(2,1)} async-done(((bf16[3072,192]{0,1:T(8,128)(2,1)}), bf16[3072,768]{0,1:T(8,128)(2,1)}) %all-gather.3.cloned.1.call-update) | async-done | bytes 4718608 | tf_op jit(solution)/shard_map/all_gather | solution.py:399
  1220.4 62.1 %reduce-scatter.27.cloned.1.call-done = f32[96,2304]{1,0:T(8,128)} async-done(((f32[768,2304]{1,0:T(8,128)}), f32[96,2304]{1,0:T(8,128)}) %reduce-scatter.27.cloned.1.call-update) | async-done | bytes 884752 | tf_op jit(solution)/shard_map/reduce_scatter | solution.py:413
  1310.6 52.2 %reduce-scatter.35.cloned.1.call-done = f32[384,768]{1,0:T(8,128)} async-done(((f32[3072,768]{1,0:T(8,128)}), f32[384,768]{1,0:T(8,128)}) %reduce-scatter.35.cloned.1.call-update) | async-done | bytes 1179664 | tf_op jit(solution)/shard_map/reduce_scatter | solution.py:416
  1372.8 83.6 %pad.19 = f32[192,4,1536]{2,0,1:T(8,128)} pad(f32[192,4,768]{2,0,1:T(8,128)} %fusion.65, f32[]{:T(128)} %constant.91.clone.1), padding=0_0_0x0_0_0x0_1_1 | pad | bytes 7077892 | tf_op jit(solution)/shard_map/pad | solution.py:96
  1465.9 84.0 %pad.20 = f32[192,4,1536]{2,0,1:T(8,128)} pad(f32[192,4,768]{2,0,1:T(8,128)} %pad_add_fusion, f32[]{:T(128)} %constant.91.clone.1), padding=0_0_0x0_0_0x1_0_1 | pad | bytes 7077892 | tf_op jit(solution)/shard_map/pad | solution.py:97
  1578.7 49.9 %all-reduce.7 = (f32[99]{0:T(128)}, f32[768]{0:T(1024)}, f32[768]{0:T(1024)}, f32[768]{0:T(1024)}, f32[768]{0:T(1024)}, /*index=5*/f32[768]{0:T(1024)}, f32[768]...) all-reduce(f32[99]{0:T(128)} %compare_select_fusion, ...), channel_id=1, replica_groups=mesh['dp'=8,'chan'=4] {'dp','chan'}, use_global_device_ids=true, to_apply=%region_13.14 | all-reduce | flops 10851 | bytes 86808 | tf_op jit(solution)/shard_map/psum | solution.py:434
  1642.0 102.7 %all-gather.5.cloned.1.call-done = bf16[768,6144]{1,0:T(8,128)(2,1)} async-done(((bf16[192,6144]{1,0:T(8,128)(2,1)}), bf16[768,6144]{1,0:T(8,128)(2,1)}) %all-gather.5.cloned.1.call-update) | async-done | bytes 9437200 | tf_op jit(solution)/shard_map/all_gather | solution.py:407
  1744.7 12.8 copy.137
  1792.7 24.8 %reduce-scatter.37.cloned.1.call-done = f32[96,60]{1,0:T(8,128)} async-done(((f32[768,60]{1,0:T(8,128)}), f32[96,60]{1,0:T(8,128)}) %reduce-scatter.37.cloned.1.call-update) | async-done | bytes 23056
  (439 shorter events, 417.7 us)
Async XLA Ops:
  7.2 639.6 %copy-start = (bf16[3,768,768]{2,1,0:T(8,128)(2,1)S(1)}, bf16[3,768,768]{2,1,0:T(8,128)(2,1)}, u32[]{:S(2)}) copy-start(bf16[3,768,768]{2,1,0:T(8,128)(2,1)} %param.29) | copy-start | bytes 10616836
  7.2 362.9 %reduce-scatter.23.cloned.1.call-start = ((), (), s32[]{:S(2)}) async-start(), calls=%async_computation.14 | async-start | bytes 23592960 | tf_op jit(solution)/shard_map/reduce_scatter | solution.py:276
  53.5 765.0 %reduce-scatter.25.cloned.1.call-start = ((), (), s32[]{:S(2)}) async-start(), calls=%async_computation.15 | async-start | bytes 11796480 | tf_op jit(solution)/shard_map/reduce_scatter | solution.py:286
  54.3 328.7 %copy-start.42 = (f32[192]{0:T(256)}, f32[192]{0:T(256)S(1)}, u32[]{:S(2)}) copy-start(f32[192]{0:T(256)S(1)} %dynamic_slice.52) | copy-start | bytes 2308
  662.6 163.6 %copy-start.44 = (f32[192]{0:T(256)}, f32[192]{0:T(256)S(1)}, u32[]{:S(2)}) copy-start(f32[192]{0:T(256)S(1)} %dynamic_slice.54) | copy-start | bytes 2308
  827.3 34.2 %all-to-all-start = ((bf16[4,768,192]{1,2,0:T(8,128)(2,1)}), bf16[4,768,192]{1,2,0:T(8,128)(2,1)}, u32[]{:S(2)}, u32[]{:S(2)}) async-start(bf16[4,768,192]{1,2,0:T(8,128)(2,1)} %bitcast.337), calls=%async_computation.2 | async-start | bytes 2359296 | tf_op jit(solution)/shard_map/all_to_all | solution.py:295
  832.0 325.3 %reduce-scatter.29.cloned.1.call-start = ((), (), s32[]{:S(2)}) async-start(), calls=%async_computation.19 | async-start | bytes 2654208 | tf_op jit(solution)/shard_map/reduce_scatter | solution.py:414
  840.9 144.9 %copy-start.34 = (f32[768]{0:T(1024)}, f32[768]{0:T(1024)S(1)}, u32[]{:S(2)}) copy-start(f32[768]{0:T(1024)S(1)} %convert_element_type.259) | copy-start | bytes 9220
  924.8 60.9 %copy-start.3 = (f32[768,768]{0,1:T(8,128)}, f32[768,768]{0,1:T(8,128)S(1)}, u32[]{:S(2)}) copy-start(f32[768,768]{0,1:T(8,128)S(1)} %get-tuple-element.284) | copy-start | bytes 7077892
  924.9 60.9 %copy-start.28 = (f32[768]{0:T(1024)}, f32[768]{0:T(1024)S(1)}, u32[]{:S(2)}) copy-start(f32[768]{0:T(1024)S(1)} %broadcast_multiply_fusion) | copy-start | bytes 9220
  926.7 59.0 %copy-start.36 = (f32[768]{0:T(1024)}, f32[768]{0:T(1024)S(1)}, u32[]{:S(2)}) copy-start(f32[768]{0:T(1024)S(1)} %fusion.93) | copy-start | bytes 9220
  996.5 76.5 %copy-start.23 = (f32[768]{0:T(1024)S(1)}, f32[768]{0:T(1024)}, u32[]{:S(2)}) copy-start(f32[768]{0:T(1024)} %copy-done.22) | copy-start | bytes 9220
  996.5 76.5 %copy-start.25 = (f32[768]{0:T(1024)S(1)}, f32[768]{0:T(1024)}, u32[]{:S(2)}) copy-start(f32[768]{0:T(1024)} %copy-done.24) | copy-start | bytes 9220
  1081.4 133.8 %all-gather.3.cloned.1.call-start = ((), (), s32[]{:S(2)}) async-start(), calls=%async_computation.16 | async-start | bytes 5898240 | tf_op jit(solution)/shard_map/all_gather | solution.py:399
  1126.6 155.9 %reduce-scatter.27.cloned.1.call-start = ((), (), s32[]{:S(2)}) async-start(), calls=%async_computation.18 | async-start | bytes 7962624 | tf_op jit(solution)/shard_map/reduce_scatter | solution.py:413
  1135.0 227.8 %reduce-scatter.35.cloned.1.call-start = ((), (), s32[]{:S(2)}) async-start(), calls=%async_computation.22 | async-start | bytes 10616832 | tf_op jit(solution)/shard_map/reduce_scatter | solution.py:416
  1145.9 404.0 %reduce-scatter.31.cloned.1.call-start = ((), (), s32[]{:S(2)}) async-start(), calls=%async_computation.20 | async-start | bytes 10616832 | tf_op jit(solution)/shard_map/reduce_scatter | solution.py:415
  1157.2 417.6 %reduce-scatter.43.cloned.1.call-start = ((), (), s32[]{:S(2)}) async-start(), calls=%async_computation.26 | async-start | bytes 245760
  1160.7 469.1 %reduce-scatter.41.cloned.1.call-start = ((), (), s32[]{:S(2)}) async-start(), calls=%async_computation.25 | async-start | bytes 737280
  1286.6 346.5 %reduce-scatter.39.cloned.1.call-start = ((), (), s32[]{:S(2)}) async-start(), calls=%async_computation.24 | async-start | bytes 2211840
  1303.8 333.0 %reduce-scatter.45.cloned.1.call-start = ((), (), s32[]{:S(2)}) async-start(), calls=%async_computation.27 | async-start | bytes 737280
  1367.1 273.2 %reduce-scatter.33.cloned.1.call-start = ((), (), s32[]{:S(2)}) async-start(), calls=%async_computation.21 | async-start | bytes 737280 | tf_op jit(solution)/shard_map/reduce_scatter | solution.py:427
  1552.1 192.6 %all-gather.5.cloned.1.call-start = ((), (), s32[]{:S(2)}) async-start(), calls=%async_computation.17 | async-start | bytes 11796480 | tf_op jit(solution)/shard_map/all_gather | solution.py:407
  1564.4 253.1 %reduce-scatter.37.cloned.1.call-start = ((), (), s32[]{:S(2)}) async-start(), calls=%async_computation.23 | async-start | bytes 442368
  (60 other events, 438.4 us)
Sparse Core Ops, SparseCore 0:
  53.7 316.4 reduce-scatter.22
  656.1 162.3 reduce-scatter.24
  1081.5 40.6 reduce-scatter.28
  1126.7 88.3 all-gather.2
  1218.5 63.9 reduce-scatter.26
  1286.3 76.4 reduce-scatter.34
  1366.7 76.4 reduce-scatter.30
  1446.1 19.3 reduce-scatter.42
  1467.7 20.1 reduce-scatter.40
  1491.2 38.6 reduce-scatter.38
  1532.3 21.9 reduce-scatter.44
  1556.6 20.2 reduce-scatter.32
  1578.5 166.0 all-gather.4
  1785.4 32.0 reduce-scatter.36
where the time goes:
time: 1840 us; the launch traced here: 1830 us
  waiting for transfers between devices  783 us (43%)
  local copies, waits for them, and re-layouts  579 us (31%)
  matrix products  255 us (14%)
  other arithmetic  107 us (6%)
  blocking collectives  81.2 us (4%)
    reduce_scatter x1, waiting for transfers between devices, on_device(): lax.psum_scatter(conv_channel_major(conv_one_w, taps_one), 'chan', scatte...  316 us
    slice x3, local copies, waits for them, and re-layouts, taps_stride_two(): padded[:, :, offset:offset + 2 * length:2].reshape(signal.shape[0], -1)  252 us
    reduce_scatter x1, waiting for transfers between devices, on_device(): lax.psum_scatter(partial_two, 'chan', scatter_dimension=1, tiled=True)  156 us
    all_gather x1, waiting for transfers between devices, on_device(): grad_one = lax.all_gather(grad_one_local, 'chan', axis=0, tiled=True)  103 us
    pad x1, local copies, waits for them, and re-layouts, stride_two_back(): odd_spread = lax.pad(odd_terms, fill, ((0, 0, 0), (0, 0, 0), (1, 0, 1)))  84 us
    pad x1, local copies, waits for them, and re-layouts, stride_two_back(): even_spread = lax.pad(parts[1], fill, ((0, 0, 0), (0, 0, 0), (0, 1, 1)))  83.6 us
    reduce_scatter x1, waiting for transfers between devices, on_device(): lax.psum_scatter(grad_w_qkv, 'dp', scatter_dimension=0, tiled=True)  62.1 us
    unnamed x166, local copies, waits for them, and re-layouts  56.7 us
  transfers between devices with their start and end apart: 15, of which 8 were waited for; matrix products, arithmetic and copies ran while one was open for 18% of the time, Pallas kernels for 0%

commit v1 on v0

v1 whole, which is shorter than its diff:
```python
import math

import jax
import jax.numpy as jnp
import numpy as np
from jax import lax
from jax.sharding import PartitionSpec as P

HEAD_DIM = 64
GROUPS = 99

bf16 = jnp.bfloat16
f32 = jnp.float32
epsilon = 1e-05
masked_score = -1e30


def gelu_exact(values):
    return jax.nn.gelu(values, approximate=False)


def normalize(values, ln_gain, ln_bias):
    average = jnp.mean(values, axis=-1, keepdims=True)
    centred = values - average
    variance = jnp.mean(centred * centred, axis=-1, keepdims=True)
    return centred * lax.rsqrt(variance + epsilon) * ln_gain + ln_bias


def sinusoids(length, channels):
    half_width = channels // 2
    increment = math.log(10000.0) / (half_width - 1)
    inverse = np.exp(-increment * np.arange(half_width, dtype=np.float64))
    angles = np.arange(length, dtype=np.float64)[:, None] * inverse[None, :]
    return np.concatenate([np.sin(angles), np.cos(angles)], axis=1).astype(np.float32)


def lookup(row_id, table):
    matches = row_id == jnp.arange(table.shape[0], dtype=jnp.int32)
    return jnp.sum(jnp.where(matches, table, 0))


def mm(a, b):
    return jnp.dot(a, b, preferred_element_type=f32)


def mm_nt(a, b):
    return lax.dot_general(a, b, (((1,), (1,)), ((), ())), preferred_element_type=f32)


def mm_tn(a, b):
    return lax.dot_general(a, b, (((0,), (0,)), ((), ())), preferred_element_type=f32)


def ahead(values):
    return jnp.pad(values[1:], ((0, 1), (0, 0)))


def behind(values):
    return jnp.pad(values[:-1], ((1, 0), (0, 0)))


def pick_frames(mel_count, offset):
    frame = lax.broadcasted_iota(jnp.int32, (mel_count, mel_count // 2), 0)
    slot = lax.broadcasted_iota(jnp.int32, (mel_count, mel_count // 2), 1)
    return (frame == 2 * slot + offset).astype(bf16)


def heads_of(block):
    return block.reshape(block.shape[0], -1, HEAD_DIM).transpose(1, 0, 2)


def from_heads(items):
    return items.transpose(1, 0, 2).reshape(items.shape[1], -1)


def attend(pieces):
    query, key, value, key_ok = pieces
    scores = mm_nt(query, key) * HEAD_DIM ** (-0.5)
    scores = jnp.where(key_ok[None, :], scores, masked_score)
    exponent = jnp.exp(scores - jnp.max(scores, axis=-1, keepdims=True))
    attention = (exponent / jnp.sum(exponent, axis=-1, keepdims=True)).astype(bf16)
    return mm(attention, value).astype(bf16), attention


def attend_back(pieces):
    query, key, value, attention, grad = pieces
    weight = attention.astype(f32)
    grad_attention = mm_nt(grad, value)
    inner = jnp.sum(weight * grad_attention, axis=-1, keepdims=True)
    grad_scores = (weight * (grad_attention - inner)).astype(bf16)
    score_scale = HEAD_DIM ** (-0.5)
    return (
        (mm(grad_scores, key) * score_scale).astype(bf16),
        (mm_tn(grad_scores, query) * score_scale).astype(bf16),
        mm_tn(attention, grad).astype(bf16),
    )


def column_sum(values):
    return jnp.sum(values.astype(f32), axis=0)


def on_device(
    mel_input,
    w_conv1,
    b_conv1,
    w_conv2,
    b_conv2,
    gain_attn,
    bias_attn,
    w_qkv,
    b_query,
    b_value,
    w_out,
    b_out,
    gain_mlp,
    bias_mlp,
    w_up,
    b_up,
    w_down,
    b_down,
    target,
    lengths,
    row_clip,
    language,
):
    clip_count, frame_count, model_width = target.shape
    mel_count = mel_input.shape[2]
    row_at = lax.axis_index("dp") * lax.axis_size("chan") + lax.axis_index("chan")
    own_id = lax.dynamic_index_in_dim(row_clip, row_at * clip_count, keepdims=False)
    valid_len = lookup(own_id, lengths)
    own_lang = lookup(own_id, language)
    frame_ok = jnp.arange(frame_count, dtype=jnp.int32) < valid_len
    wide = lambda v: v.astype(f32)

    mel = lax.all_to_all(mel_input, "chan", split_axis=1, concat_axis=0, tiled=True)[:, 0]
    pick_even, pick_odd = pick_frames(mel_count, 0), pick_frames(mel_count, 1)
    mel_even = mm_tn(pick_even, mel.T).astype(bf16)
    mel_odd = mm_tn(pick_odd, mel.T).astype(bf16)
    taps_even = (behind(mel_odd), mel_even, mel_odd)
    taps_odd = (mel_even, mel_odd, ahead(mel_even))
    one_even = sum(mm(taps_even[j], w_conv1[j]) for j in range(3)) + wide(b_conv1)
    one_odd = sum(mm(taps_odd[j], w_conv1[j]) for j in range(3)) + wide(b_conv1)
    act_even, pull_even = jax.vjp(gelu_exact, one_even)
    act_odd, pull_odd = jax.vjp(gelu_exact, one_odd)
    act_even, act_odd = act_even.astype(bf16), act_odd.astype(bf16)
    taps_two = (behind(act_odd), act_even, act_odd)
    conv_two = sum(mm(taps_two[j], w_conv2[j]) for j in range(3)) + wide(b_conv2)
    act_two, pull_two = jax.vjp(gelu_exact, conv_two)
    stem = (act_two + sinusoids(frame_count, model_width)).astype(bf16)
    stem_float = stem.astype(f32)
    normed_a, norm_a_pull = jax.vjp(normalize, stem_float, wide(gain_attn), wide(bias_attn))
    normed_a = normed_a.astype(bf16)
    flat_zero = jnp.zeros((model_width,), f32)
    qkv_bias = jnp.concatenate([wide(b_query), flat_zero, wide(b_value)])
    joined = (mm(normed_a, w_qkv) + qkv_bias).astype(bf16)
    query, key, value = (
        heads_of(joined[:, i * model_width : (i + 1) * model_width]) for i in range(3)
    )
    head_count = query.shape[0]
    context, attention = lax.map(
        attend, (query, key, value, jnp.broadcast_to(frame_ok, (head_count, frame_count)))
    )
    context = from_heads(context)
    middle = stem_float + mm(context, w_out) + wide(b_out)
    normed_b, norm_b_pull = jax.vjp(normalize, middle, wide(gain_mlp), wide(bias_mlp))
    normed_b = normed_b.astype(bf16)
    upward = mm(normed_b, w_up) + wide(b_up)
    hidden, pull_up = jax.vjp(gelu_exact, upward)
    hidden = hidden.astype(bf16)
    final_rows = middle + mm(hidden, w_down) + wide(b_down)
    mismatch = jnp.where(frame_ok[:, None], final_rows - target[0].astype(f32), 0.0)
    clip_loss = 0.5 * jnp.sum(mismatch * mismatch)
    group_ids = jnp.arange(GROUPS, dtype=jnp.int32)
    group_part = jnp.where(own_lang == group_ids, clip_loss, 0.0)

    grad_branch = mismatch.astype(bf16)
    grad_b_down = column_sum(grad_branch)
    grad_w_down = mm_tn(hidden, grad_branch).astype(bf16)
    grad_up = pull_up(mm_nt(grad_branch, w_down))[0].astype(bf16)
    grad_b_up = column_sum(grad_up)
    grad_w_up = mm_tn(normed_b, grad_up).astype(bf16)
    grad_mid_norm, grad_gain_mlp, grad_bias_mlp = norm_b_pull(mm_nt(grad_up, w_up))
    grad_middle = mismatch + grad_mid_norm
    grad_attended = grad_middle.astype(bf16)
    grad_b_out = column_sum(grad_attended)
    grad_w_out = mm_tn(context, grad_attended).astype(bf16)
    grad_context = heads_of(mm_nt(grad_attended, w_out).astype(bf16))
    grads = lax.map(attend_back, (query, key, value, attention, grad_context))
    grad_joined = jnp.concatenate([from_heads(g) for g in grads], axis=1)
    grad_b_query = column_sum(grad_joined[:, :model_width])
    grad_b_value = column_sum(grad_joined[:, 2 * model_width :])
    grad_w_qkv = mm_tn(normed_a, grad_joined).astype(bf16)
    grad_stem_norm, grad_gain_attn, grad_bias_attn = norm_a_pull(mm_nt(grad_joined, w_qkv))
    grad_stem = (grad_middle + grad_stem_norm).astype(bf16)
    grad_two = pull_two(grad_stem.astype(f32))[0].astype(bf16)
    grad_b_two = column_sum(grad_two)
    grad_w_two = jnp.stack([mm_tn(taps_two[j], grad_two).astype(bf16) for j in range(3)])
    grad_act_even = mm_nt(grad_two, w_conv2[1])
    grad_act_odd = mm_nt(grad_two, w_conv2[2]) + mm_nt(ahead(grad_two), w_conv2[0])
    grad_even = pull_even(grad_act_even)[0].astype(bf16)
    grad_odd = pull_odd(grad_act_odd)[0].astype(bf16)
    grad_b_one = column_sum(grad_even) + column_sum(grad_odd)
    grad_w_one = jnp.stack(
        [
            (mm_tn(taps_even[j], grad_even) + mm_tn(taps_odd[j], grad_odd)).astype(bf16)
            for j in range(3)
        ]
    )
    grad_mel_even = (
        mm_nt(grad_odd, w_conv1[0]) + mm_nt(grad_even, w_conv1[1]) + mm_nt(behind(grad_odd), w_conv1[2])
    )
    grad_mel_odd = (
        mm_nt(ahead(grad_even), w_conv1[0]) + mm_nt(grad_odd, w_conv1[1]) + mm_nt(grad_even, w_conv1[2])
    )
    back_mel = (
        lax.dot_general(grad_mel_even.astype(bf16), pick_even, (((0,), (1,)), ((), ())), preferred_element_type=f32)
        + lax.dot_general(grad_mel_odd.astype(bf16), pick_odd, (((0,), (1,)), ((), ())), preferred_element_type=f32)
    ).astype(bf16)
    grad_mel = lax.all_to_all(back_mel[:, None], "chan", split_axis=0, concat_axis=1, tiled=True)

    def scatter(values, dp_at, chan_at):
        part = lax.psum_scatter(values, "dp", scatter_dimension=dp_at, tiled=True)
        return lax.psum_scatter(part, "chan", scatter_dimension=chan_at, tiled=True).astype(f32)

    final_down = scatter(grad_w_down, 0, 1)
    final_up = scatter(grad_w_up, 0, 1)
    final_out = scatter(grad_w_out, 0, 1)
    final_qkv = scatter(grad_w_qkv, 0, 1)
    part_two = scatter(grad_w_two, 2, 1)
    part_one = scatter(grad_w_one, 2, 1)
    totals_all = lax.psum(
        (
            group_part,
            grad_b_one,
            grad_b_two,
            grad_gain_attn,
            grad_bias_attn,
            grad_b_query,
            grad_b_value,
            grad_b_out,
            grad_gain_mlp,
            grad_bias_mlp,
            grad_b_up,
            grad_b_down,
        ),
        ("dp", "chan"),
    )
    member_all = language[:, None] == group_ids[None, :]
    frames_group = jnp.sum(jnp.where(member_all, lengths[:, None], 0), axis=0)
    group_loss = totals_all[0] / (model_width * jnp.maximum(frames_group, 1).astype(f32))
    block_out = final_rows.astype(bf16).reshape(clip_count, frame_count, model_width)
    return (
        block_out,
        group_loss,
        grad_mel,
        part_one,
        totals_all[1],
        part_two,
        totals_all[2],
        totals_all[3],
        totals_all[4],
        final_qkv,
        totals_all[5],
        totals_all[6],
        final_out,
        totals_all[7],
        totals_all[8],
        totals_all[9],
        final_up,
        totals_all[10],
        final_down,
        totals_all[11],
    )


def solution(mesh):
    whole = P()
    by_row = P(("dp", "chan"), None, None)
    return jax.shard_map(
        on_device,
        mesh=mesh,
        in_specs=(P("chan", "dp", None),) + (whole,) * 17 + (by_row,) + (whole,) * 3,
        out_specs=(
            by_row,
            whole,
            P("chan", "dp", None),
            P(None, "chan", "dp"),
            whole,
            P(None, "chan", "dp"),
            whole,
            whole,
            whole,
            P("dp", "chan"),
            whole,
            whole,
            P("dp", "chan"),
            whole,
            whole,
            whole,
            P("dp", "chan"),
            whole,
            P("dp", "chan"),
            whole,
        ),
        check_vma=False,
    )
```

time: 1840 us -> 757 us (0.41)
  waiting for transfers between devices: 783 us -> 163 us
  local copies, waits for them, and re-layouts: 579 us -> 91.2 us
  matrix products: 255 us -> 306 us
  blocking collectives: 81.2 us -> 62.4 us
    reduce_scatter x7 -> x6, waiting for transfers between devices: 586 us -> 119 us  [the longest x4 99.4 us: scatter(): part = lax.psum_scatter(values, 'dp', scatter_dimension=dp_at, tiled=True)]
    slice x8 -> x7, local copies, waits for them, and re-layouts: 264 us -> 13.4 us  [the longest x4 8.98 us: on_device(): joined[:, i * model_width:(i + 1) * model_width]]
    pad x3 -> x0, local copies, waits for them, and re-layouts: 173 us -> none  [the longest x1 84 us: stride_two_back(): odd_spread = lax.pad(odd_terms, fill, ((0, 0, 0), (0, 0, 0), (1, 0, 1)))]
    all_gather x2 -> x0, waiting for transfers between devices: 157 us -> none  [the longest x1 103 us: on_device(): grad_one = lax.all_gather(grad_one_local, 'chan', axis=0, tiled=True)]
    dot_general x72 -> x113, matrix products: 255 us -> 306 us  [the longest x37 119 us: mm(): return jnp.dot(a, b, preferred_element_type=f32)]
    dynamic_slice x51 -> x13, local copies, waits for them, and re-layouts: 36.3 us -> 1.58 us  [the longest x1 1.24 us: on_device(): lax.dynamic_index_in_dim(row_clip, row_at * clip_count, keepdims=False)]
    all_to_all x1 -> x0, blocking collectives: 31.3 us -> none  [on_device(): lax.all_to_all(grad_stem, 'chan', split_axis=1, concat_axis=0, tiled=True)]
    unnamed x0 -> x1, blocking collectives: none -> 20.5 us
  transfers between devices with their start and end apart: 15 -> 13, of which waited for: 8 -> 5; matrix products, arithmetic and copies ran while one was open for 18% -> 38% of each run, Pallas kernels for 0% -> 0%
where the time goes in v1:
time: 757 us; the launch traced here: 748 us
  matrix products  306 us (40%)
  waiting for transfers between devices  163 us (22%)
  other arithmetic  97.7 us (13%)
  local copies, waits for them, and re-layouts  91.2 us (12%)
  blocking collectives  62.4 us (8%)
  between operations  16.1 us (2%)
  starting transfers between devices  11.9 us (2%)
    dot_general x37, matrix products, mm(): return jnp.dot(a, b, preferred_element_type=f32)  119 us
    reduce_scatter x4, waiting for transfers between devices, scatter(): part = lax.psum_scatter(values, 'dp', scatter_dimension=dp_at, tiled=True)  99.4 us
    dot_general x39, matrix products, mm_tn(): lax.dot_general(a, b, (((0,), (0,)), ((), ())), preferred_element_type=f32)  92.5 us
    dot_general x35, matrix products, mm_nt(): lax.dot_general(a, b, (((1,), (1,)), ((), ())), preferred_element_type=f32)  87.1 us
    unnamed x160, local copies, waits for them, and re-layouts  52 us
    unnamed x16, waiting for transfers between devices  44.2 us
    psum x1, blocking collectives, on_device(): lax.psum((group_part, grad_b_one, grad_b_two, grad_gain_attn, grad_bias_a...  41.8 us
    unnamed x1, blocking collectives  20.5 us
  transfers between devices with their start and end apart: 13, of which 5 were waited for; matrix products, arithmetic and copies ran while one was open for 38% of the time, Pallas kernels for 0%

profile of v1, /device:TPU:0, one launch (start us, length us, event | category | flops | bytes accessed | tf_op | source)
XLA Modules:
  0.0 748.3 jit_solution(8251982566000432357)
XLA Ops:
  9.1 6.3 all-to-all-start
  41.4 7.4 multiply_convert_fusion.2
  49.8 7.2 multiply_convert_fusion.1
  59.1 7.5 %convert_reduce_fusion.1 = (f32[768]{0:T(1024)S(1)}, bf16[768,768]{1,0:T(8,128)(2,1)S(1)}, f32[768,768]{1,0:T(8,128)}) fusion(f32[768,768]{1,0:T(8,128)S(1)} %copy-done.57, f32[768]{0:T(1024)S(1)} %copy-done.45, bf16[768,768]{1,0:T(8,128)(2,1)S(1)} %get-tuple-element.306, bf16[3,768,768]{2,1,0:T(8,128)(2,1)S(1)} %copy-done.54, f32[768,768]{1,0:T(8,128)S(1)} %fusion.117, ...), kind=kOutput, calls=%fused_computation.86 | convolution fusion | flops 947846400 | bytes 12983296 | tf_op jit(solution)/shard_map/dot_general | solution.py:43
  92.5 73.5 %while.26 = (s32[]{:T(128)}, bf16[12,768,64]{1,2,0:T(8,128)(2,1)}, bf16[12,768,768]{1,2,0:T(8,128)(2,1)}, pred[12,768]{1,0:T(8,128)(4,1)S(1)}, bf16[12,768,64]{2...) while((s32[]{:T(128)}, bf16[12,768,64]{1,2,0:T(8,128)(2,1)}, ...), condition=%wide.region_6.7_spmd, body=%wide.region_3.6_spmd.sunk | while | flops 161069568 | bytes 11333721 | solution.py:161
  171.2 26.8 %multiply_convert_fusion = (bf16[768,3072]{1,0:T(8,128)(2,1)S(1)}, f32[768,3072]{1,0:T(8,128)}, f32[768,3072]{1,0:T(8,128)}) fusion(f32[3072]{0:T(1024)S(1)} %copy-done.39, bf16[768,3072]{1,0:T(8,128)(2,1)S(1)} %bitcast.298, f32[768,768]{1,0:T(8,128)S(1)} %get-tuple-element.320, f32[768]{0:T(1024)S(1)} %copy-done.40, f32[768]{0:T(1024)S(1)} %copy-done.35, ...), kind=kOutput, calls=%fused_computation.56 | convolution fusion | flops 3782541312 | bytes 30695424 | tf_op jit(solution)/shard_map/dot_general | solution.py:43
  198.1 5.8 convert_reduce_fusion.2
  203.8 13.7 %convert_reduce_fusion = (f32[3072]{0:T(1024)}, bf16[768,3072]{1,0:T(8,128)(2,1)}) fusion(f32[768,3072]{1,0:T(8,128)} %get-tuple-element.301, bf16[3072,768]{1,0:T(8,128)(2,1)S(1)} %bitcast.296, f32[768,768]{1,0:T(8,128)S(1)} %get-tuple-element.299, f32[768,3072]{1,0:T(8,128)} %get-tuple-element.321, f32[3072]{0:T(1024)S(1)} %copy-done.39), kind=kOutput, calls=%fused_computation.54 | convolution fusion | flops 3664573440 | bytes 30695424 | tf_op jit(solution)/shard_map/dot_general | solution.py:47
  217.5 8.2 %multiply_reduce_fusion = (f32[768]{0:T(1024)}, f32[768]{0:T(1024)S(1)}, f32[768]{0:T(1024)}, f32[768,768]{1,0:T(8,128)S(1)}) fusion(f32[768,768]{1,0:T(8,128)S(1)} %get-tuple-element.320, f32[768]{0:T(1024)S(1)} %fusion.202, f32[768]{0:T(1024)S(1)} %broadcast_multiply_fusion, f32[768]{0:T(1024)S(1)} %copy-done.35, ...), kind=kOutput, calls=%fused_computation.118 | convolution fusion | flops 3628594944 | bytes 14174208 | tf_op jit(solution)/shard_map/dot_general | solution.py:47
  243.7 122.1 %while.27 = (s32[]{:T(128)}, bf16[12,768,64]{1,2,0:T(8,128)(2,1)}, bf16[12,768,64]{1,2,0:T(8,128)(2,1)}, bf16[12,768,64]{1,2,0:T(8,128)(2,1)}, bf16[12,768,768]{...) while((s32[]{:T(128)}, bf16[12,768,64]{1,2,0:T(8,128)(2,1)}, ...), condition=%wide.region_17.18_spmd, body=%wide.region_15.17_spmd.sunk | while | flops 306363648 | bytes 13085801 | solution.py:189
  365.7 7.5 convolution_convert_fusion.1
  373.3 6.5 fusion.226
  381.6 7.9 %convert_reduce_fusion.6 = (f32[768]{0:T(1024)}, bf16[768,768]{1,0:T(8,128)(2,1)S(1)}) fusion(f32[768,768]{1,0:T(8,128)S(1)} %copy-done.20, f32[768]{0:T(1024)S(1)} %negate_multiply_fusion.4, f32[768]{0:T(1024)S(1)} %multiply_multiply_fusion.20, f32[768]{0:T(1024)S(1)} %copy-done.26, bf16[768,768]{1,0:T(8,128)(2,1)S(1)} %copy-done.8, ...), kind=kLoop, calls=%fused_computation.122 | loop fusion | flops 51313920 | bytes 11817984 | tf_op jit(solution)/shard_map/reduce_sum | solution.py:100
  395.0 8.3 %copy.109 = bf16[3,768,768]{1,0,2:T(4,128)(2,1)} copy(bf16[3,768,768]{2,1,0:T(8,128)(2,1)} %pad_maximum_fusion.1) | data formatting | bytes 7077888
  408.3 9.3 %convolution_convert_fusion.2 = bf16[3072,768]{1,0:T(8,128)(2,1)} fusion(bf16[768,3072]{1,0:T(8,128)(2,1)} %copy-done.65, f32[768,768]{1,0:T(8,128)} %copy-done.10), kind=kOutput, calls=%fused_computation.72 | convolution fusion | flops 3626827776 | bytes 11796480 | tf_op jit(solution)/shard_map/dot_general | solution.py:51
  418.2 9.5 %convolution_convert_fusion.3 = bf16[768,3072]{1,0:T(8,128)(2,1)} fusion(bf16[768,3072]{1,0:T(8,128)(2,1)} %get-tuple-element.329, f32[768,768]{1,0:T(8,128)} %copy-done.9, f32[768]{0:T(1024)S(1)} %copy-done.41, f32[768]{0:T(1024)S(1)} %copy-done.36, f32[768]{0:T(1024)S(1)} %copy-done.38, f32[768]{0:T(1024)S(1)} %broadcast_multiply_fusion), kind=kOutput, calls=%fused_computation.73 | convolution fusion | flops 3629187072 | bytes 11808768 | tf_op jit(solution)/shard_map/dot_general | solution.py:51
  429.5 5.3 convert_reduce_fusion.8
  451.8 23.1 %reduce-scatter.37.cloned.1.call-done = bf16[96,2304]{1,0:T(8,128)(2,1)} async-done(((bf16[768,2304]{1,0:T(8,128)(2,1)}), bf16[96,2304]{1,0:T(8,128)(2,1)}) %reduce-scatter.37.cloned.1.call-update) | async-done | bytes 442384
  479.3 53.2 %reduce-scatter.33.cloned.1.call-done = bf16[384,768]{1,0:T(8,128)(2,1)} async-done(((bf16[3072,768]{1,0:T(8,128)(2,1)}), bf16[384,768]{1,0:T(8,128)(2,1)}) %reduce-scatter.33.cloned.1.call-update) | async-done | bytes 589840 | tf_op jit(solution)/shard_map/reduce_scatter | solution.py:223
  543.6 46.2 %reduce-scatter.29.cloned.1.call-done = bf16[96,3072]{1,0:T(8,128)(2,1)} async-done(((bf16[768,3072]{1,0:T(8,128)(2,1)}), bf16[96,3072]{1,0:T(8,128)(2,1)}) %reduce-scatter.29.cloned.1.call-update) | async-done | bytes 589840 | tf_op jit(solution)/shard_map/reduce_scatter | solution.py:223
  612.0 41.8 %all-reduce.7 = (f32[99]{0:T(128)S(1)}, f32[768]{0:T(1024)}, f32[768]{0:T(1024)}, f32[768]{0:T(1024)}, f32[768]{0:T(1024)}, /*index=5*/f32[768]{0:T(1024)}, f32[...) all-reduce(f32[99]{0:T(128)S(1)} %compare_select_fusion, ...), channel_id=1, replica_groups=mesh['dp'=8,'chan'=4] {'dp','chan'}, use_global_device_ids=true, to_apply=%region_11.12 | all-reduce | flops 10851 | bytes 86808 | tf_op jit(solution)/shard_map/psum | solution.py:232
  666.5 20.5 %all-reduce.6 = bf16[3,80,96]{2,1,0:T(8,128)(2,1)} all-reduce(bf16[3,80,96]{2,1,0:T(8,128)(2,1)} %copy.106), channel_id=3, replica_groups=mesh['dp'=8,'chan'=4] {'chan'}, use_global_device_ids=true, to_apply=%region_21.22.clone | all-reduce | flops 23040 | bytes 92160
  696.3 20.9 %reduce-scatter.43.cloned.1.call-done = bf16[192,384]{1,0:T(8,128)(2,1)} async-done(((bf16[768,384]{1,0:T(8,128)(2,1)}), bf16[192,384]{1,0:T(8,128)(2,1)}) %reduce-scatter.43.cloned.1.call-update) | async-done | bytes 147472
  720.7 19.2 %reduce-scatter.31.cloned.1.call-done = bf16[96,768]{1,0:T(8,128)(2,1)} async-done(((bf16[96,3072]{1,0:T(8,128)(2,1)}), bf16[96,768]{1,0:T(8,128)(2,1)}) %reduce-scatter.31.cloned.1.call-update) | async-done | bytes 147472 | tf_op jit(solution)/shard_map/reduce_scatter | solution.py:224
  (409 shorter events, 369.6 us)
Async XLA Ops:
  7.2 60.6 %copy-start = (bf16[768,2304]{1,0:T(8,128)(2,1)S(1)}, bf16[768,2304]{1,0:T(8,128)(2,1)}, u32[]{:S(2)}) copy-start(bf16[768,2304]{1,0:T(8,128)(2,1)} %param.34) | copy-start | bytes 10616836
  9.1 24.3 %all-to-all-start = ((bf16[20,4,1536]{2,0,1:T(8,128)(2,1)}), bf16[20,4,1536]{2,0,1:T(8,128)(2,1)}, u32[]{:S(2)}, u32[]{:S(2)}) async-start(bf16[20,4,1536]{2,0,1:T(8,128)(2,1)} %copy.85), calls=%async_computation | async-start | bytes 589824 | tf_op jit(solution)/shard_map/all_to_all | solution.py:136
  15.4 432.3 %reduce-scatter.27.cloned.1.call-start = ((), (), s32[]{:S(2)}) async-start(), calls=%async_computation.15 | async-start | bytes 1327104 | tf_op jit(solution)/shard_map/reduce_scatter | solution.py:223
  92.5 73.5 %copy-start.44 = (f32[768]{0:T(1024)S(1)}, f32[768]{0:T(1024)}, u32[]{:S(2)}) copy-start(f32[768]{0:T(1024)} %convert_element_type.233) | copy-start | bytes 9220
  169.5 56.3 %copy-start.9 = (f32[768,768]{1,0:T(8,128)}, f32[768,768]{1,0:T(8,128)S(1)}, u32[]{:S(2)}) copy-start(f32[768,768]{1,0:T(8,128)S(1)} %get-tuple-element.320) | copy-start | bytes 7077892
  171.2 54.6 %copy-start.37 = (f32[768]{0:T(1024)}, f32[768]{0:T(1024)S(1)}, u32[]{:S(2)}) copy-start(f32[768]{0:T(1024)S(1)} %fusion.202) | copy-start | bytes 9220
  236.3 213.3 %reduce-scatter.25.cloned.1.call-start = ((), (), s32[]{:S(2)}) async-start(), calls=%async_computation.14 | async-start | bytes 3981312 | tf_op jit(solution)/shard_map/reduce_scatter | solution.py:223
  243.7 122.1 %copy-start.26 = (f32[768]{0:T(1024)S(1)}, f32[768]{0:T(1024)}, u32[]{:S(2)}) copy-start(f32[768]{0:T(1024)} %copy-done.25) | copy-start | bytes 9220
  243.7 122.1 %copy-start.28 = (f32[768]{0:T(1024)S(1)}, f32[768]{0:T(1024)}, u32[]{:S(2)}) copy-start(f32[768]{0:T(1024)} %copy-done.27) | copy-start | bytes 9220
  243.7 122.1 %copy-start.30 = (f32[768]{0:T(1024)S(1)}, f32[768]{0:T(1024)}, u32[]{:S(2)}) copy-start(f32[768]{0:T(1024)} %copy-done.29) | copy-start | bytes 9220
  373.2 101.7 %reduce-scatter.37.cloned.1.call-start = ((), (), s32[]{:S(2)}) async-start(), calls=%async_computation.20 | async-start | bytes 3981312
  408.2 124.3 %reduce-scatter.33.cloned.1.call-start = ((), (), s32[]{:S(2)}) async-start(), calls=%async_computation.18 | async-start | bytes 5308416 | tf_op jit(solution)/shard_map/reduce_scatter | solution.py:223
  417.6 172.2 %reduce-scatter.29.cloned.1.call-start = ((), (), s32[]{:S(2)}) async-start(), calls=%async_computation.16 | async-start | bytes 5308416 | tf_op jit(solution)/shard_map/reduce_scatter | solution.py:223
  427.8 235.6 %reduce-scatter.35.cloned.1.call-start = ((), (), s32[]{:S(2)}) async-start(), calls=%async_computation.19 | async-start | bytes 442368
  447.6 240.8 %reduce-scatter.41.cloned.1.call-start = ((), (), s32[]{:S(2)}) async-start(), calls=%async_computation.22 | async-start | bytes 245760
  449.5 241.9 %reduce-scatter.39.cloned.1.call-start = ((), (), s32[]{:S(2)}) async-start(), calls=%async_computation.21 | async-start | bytes 737280
  451.7 83.2 %copy-start.60 = (u32[32]{0:T(128)S(1)}, u32[32]{0:T(128)}, u32[]{:S(2)}) copy-start(u32[32]{0:T(128)} %constant.199) | copy-start | bytes 388
  451.7 84.4 %copy-start.52 = (s32[32]{0:T(128)S(1)}, s32[32]{0:T(128)}, u32[]{:S(2)}) copy-start(s32[32]{0:T(128)} %param.46) | copy-start | bytes 388
  451.7 84.4 %copy-start.53 = (s32[32]{0:T(128)S(1)}, s32[32]{0:T(128)}, u32[]{:S(2)}) copy-start(s32[32]{0:T(128)} %param.48) | copy-start | bytes 388
  451.7 243.0 %reduce-scatter.23.cloned.1.call-start = ((), (), s32[]{:S(2)}) async-start(), calls=%async_computation.13 | async-start | bytes 737280 | tf_op jit(solution)/shard_map/reduce_scatter | solution.py:224
  479.3 238.0 %reduce-scatter.43.cloned.1.call-start = ((), (), s32[]{:S(2)}) async-start(), calls=%async_computation.23 | async-start | bytes 737280
  534.7 205.3 %reduce-scatter.31.cloned.1.call-start = ((), (), s32[]{:S(2)}) async-start(), calls=%async_computation.17 | async-start | bytes 737280 | tf_op jit(solution)/shard_map/reduce_scatter | solution.py:224
  542.4 51.0 %copy-start.47 = (s32[768]{0:T(1024)S(1)}, s32[768]{0:T(1024)}, u32[]{:S(2)}) copy-start(s32[768]{0:T(1024)} %iota_multiply_fusion) | copy-start | bytes 9220
  601.7 53.3 %all-to-all-start.1 = ((bf16[4,2,15360]{2,1,0:T(2,128)(2,1)}), bf16[4,2,15360]{2,1,0:T(2,128)(2,1)}, u32[]{:S(2)}, u32[]{:S(2)}) async-start(bf16[4,2,15360]{2,1,0:T(2,128)(2,1)} %reshape.176), calls=%async_computation.1 | async-start | bytes 491520 | tf_op jit(solution)/shard_map/all_to_all | solution.py:220
  (59 other events, 437.8 us)
Sparse Core Ops, SparseCore 0:
  236.4 38.2 reduce-scatter.26
  373.4 49.4 reduce-scatter.24
  426.8 48.0 reduce-scatter.36
  478.6 53.8 reduce-scatter.32
  535.8 53.9 reduce-scatter.28
  593.0 33.7 reduce-scatter.34
  629.7 19.3 reduce-scatter.40
  651.4 20.1 reduce-scatter.38
  673.9 20.1 reduce-scatter.22
  696.3 20.9 reduce-scatter.42
  719.5 20.3 reduce-scatter.30

commit v2 on v1

v2 whole, which is shorter than its diff:
```python
import math

import jax
import jax.numpy as jnp
import numpy as np
from jax import lax
from jax.experimental import pallas as pl
from jax.experimental.pallas import tpu as pltpu
from jax.sharding import PartitionSpec as P

HEAD_DIM = 64
GROUPS = 99

bf16 = jnp.bfloat16
f32 = jnp.float32
epsilon = 1e-05
masked_score = -1e30


def sinusoids(length, channels):
    half_width = channels // 2
    increment = math.log(10000.0) / (half_width - 1)
    inverse = np.exp(-increment * np.arange(half_width, dtype=np.float64))
    angles = np.arange(length, dtype=np.float64)[:, None] * inverse[None, :]
    return np.concatenate([np.sin(angles), np.cos(angles)], axis=1).astype(np.float32)


def lookup(row_id, table):
    matches = row_id == jnp.arange(table.shape[0], dtype=jnp.int32)
    return jnp.sum(jnp.where(matches, table, 0))


def mm(a, b):
    return jnp.dot(a, b, preferred_element_type=f32)


def mm_nt(a, b):
    return lax.dot_general(a, b, (((1,), (1,)), ((), ())), preferred_element_type=f32)


def mm_tn(a, b):
    return lax.dot_general(a, b, (((0,), (0,)), ((), ())), preferred_element_type=f32)


BLOCK = 256
VMEM_LIMIT = 60 * 1024 * 1024
TAIL_RATE = 0.31
TAIL = (
    0.12366556625478936,
    0.12390820374862553,
    0.10876305868035366,
    0.10683424297390944,
    -0.008837395578103507,
    0.14867850286492648,
    -0.13802626195746664,
    0.0350141511339579,
)


def gelu_pair(v):
    size = jnp.abs(v)
    base = 1.0 + TAIL_RATE * size
    rough = pl.reciprocal(base, approx=True)
    t = rough * (2.0 - base * rough)
    total = jnp.full_like(t, TAIL[-1])
    for coefficient in TAIL[-2::-1]:
        total = total * t + coefficient
    bell = jnp.exp(-0.5 * (v * v))
    tail = total * t * bell
    phi = jnp.where(v < 0.0, tail, 1.0 - tail)
    return v * phi, phi + v * (bell * (1.0 / math.sqrt(2.0 * math.pi)))


def turned(values):
    return values.astype(f32).T.astype(bf16)


def chunks(length, size):
    return [slice(at, min(at + size, length)) for at in range(0, length, size)]


def attend_kernel(len_ref, q_ref, k_ref, v_ref, ctx_ref, et_ref, inv_ref):
    length, width = q_ref.shape
    lane = lax.broadcasted_iota(jnp.int32, (length, width), 1)
    frame = lax.broadcasted_iota(jnp.int32, (length, width), 0)
    bias = jnp.where(frame < len_ref[0], 0.0, masked_score)
    q = q_ref[...].astype(f32) * HEAD_DIM ** (-0.5)
    k = k_ref[...].astype(f32)
    v_t = turned(v_ref[...])
    found = [[] for _ in chunks(length, BLOCK)]
    for h in range(2):
        mine = lane // HEAD_DIM == h
        spare = lane == HEAD_DIM * (1 - h)
        own_q = jnp.where(mine, q, jnp.where(spare, 1.0, 0.0)).astype(bf16)
        own_k = jnp.where(mine, k, jnp.where(spare, bias, 0.0)).astype(bf16)
        for at, cols in enumerate(chunks(length, BLOCK)):
            scores = mm_nt(own_k, own_q[cols])
            weight = jnp.exp(scores - jnp.max(scores, axis=0, keepdims=True))
            inverse = 1.0 / jnp.sum(weight, axis=0, keepdims=True)
            weight = weight.astype(bf16)
            et_ref[h, :, cols] = weight
            inv_ref[h, :, cols] = inverse
            found[at].append(mm(v_t[h * HEAD_DIM : (h + 1) * HEAD_DIM], weight) * inverse)
    for at, cols in enumerate(chunks(length, BLOCK)):
        ctx_ref[cols, :] = jnp.concatenate(found[at], axis=0).T.astype(bf16)


def attend_back_kernel(
    q_ref, k_ref, v_ref, et_ref, inv_ref, gctx_ref, ctx_ref, dq_ref, dk_ref, dv_ref, sums_ref, ds_ref
):
    length, width = q_ref.shape
    lane = lax.broadcasted_iota(jnp.int32, (length, width), 1)
    row = lax.broadcasted_iota(jnp.int32, (width, length), 0)
    scale = HEAD_DIM ** (-0.5)
    grad_t = gctx_ref[...].astype(f32).T * jnp.where(row < HEAD_DIM, inv_ref[0], inv_ref[1])
    grad_t = grad_t.astype(bf16).astype(f32)
    grad = grad_t.T
    inner_all = grad_t * ctx_ref[...].astype(f32).T
    k_t = turned(k_ref[...])
    q = q_ref[...].astype(f32) * scale
    v = v_ref[...].astype(f32)
    dq_t = []
    dk = jnp.zeros((length, width), f32)
    dv = jnp.zeros((length, width), f32)
    for h in range(2):
        at = HEAD_DIM * (1 - h)
        mine = lane // HEAD_DIM == h
        inner = jnp.sum(inner_all[h * HEAD_DIM : (h + 1) * HEAD_DIM], axis=0, keepdims=True)
        high = inner.astype(bf16).astype(f32)
        own_grad_t = jnp.where(row // HEAD_DIM == h, grad_t, 0.0)
        own_grad_t = jnp.where(row == at, -high, jnp.where(row == at + 1, high - inner, own_grad_t))
        own_grad_t = own_grad_t.astype(bf16)
        own_v = jnp.where(mine, v, jnp.where((lane == at) | (lane == at + 1), 1.0, 0.0)).astype(bf16)
        own_q = jnp.where(mine, q, 0.0).astype(bf16)
        own_grad = jnp.where(mine, grad, 0.0).astype(bf16)
        for cols in chunks(length, BLOCK):
            shifted = mm(own_v, own_grad_t[:, cols])
            ds_ref[:, cols] = (et_ref[h, :, cols].astype(f32) * shifted).astype(bf16)
        dk += mm(ds_ref[...], own_q)
        dv += mm(et_ref[h], own_grad)
        dq_t.append(mm(k_t[h * HEAD_DIM : (h + 1) * HEAD_DIM], ds_ref[...]))
    dq = (jnp.concatenate(dq_t, axis=0).T * scale).astype(bf16)
    dv = dv.astype(bf16)
    dq_ref[...] = dq
    dk_ref[...] = dk.astype(bf16)
    dv_ref[...] = dv
    sums_ref[0:1] = jnp.sum(dq.astype(f32), axis=0, keepdims=True)
    sums_ref[1:2] = jnp.sum(dv.astype(f32), axis=0, keepdims=True)


def attend(joined, valid_len):
    length, width = joined.shape[0], 2 * HEAD_DIM
    pairs = joined.shape[1] // (3 * width)
    block = lambda part: pl.BlockSpec((length, width), lambda p, n: (0, part * pairs + p))
    return pl.pallas_call(
        attend_kernel,
        grid_spec=pltpu.PrefetchScalarGridSpec(
            num_scalar_prefetch=1,
            grid=(pairs,),
            in_specs=[block(0), block(1), block(2)],
            out_specs=[
                block(0),
                pl.BlockSpec((2, length, length), lambda p, n: (p, 0, 0)),
                pl.BlockSpec((2, 1, length), lambda p, n: (p, 0, 0)),
            ],
        ),
        out_shape=[
            jax.ShapeDtypeStruct((length, pairs * width), bf16),
            jax.ShapeDtypeStruct((2 * pairs, length, length), bf16),
            jax.ShapeDtypeStruct((2 * pairs, 1, length), f32),
        ],
        compiler_params=pltpu.CompilerParams(vmem_limit_bytes=VMEM_LIMIT),
        name="attend",
    )(valid_len, joined, joined, joined)


def attend_back(joined, et, inverse, grad_context, context):
    length, width = joined.shape[0], 2 * HEAD_DIM
    pairs = joined.shape[1] // (3 * width)
    block = lambda part: pl.BlockSpec((length, width), lambda p: (0, part * pairs + p))
    one = jax.ShapeDtypeStruct((length, pairs * width), bf16)
    return pl.pallas_call(
        attend_back_kernel,
        grid=(pairs,),
        in_specs=[
            block(0),
            block(1),
            block(2),
            pl.BlockSpec((2, length, length), lambda p: (p, 0, 0)),
            pl.BlockSpec((2, 1, length), lambda p: (p, 0, 0)),
            block(0),
            block(0),
        ],
        out_specs=[block(0), block(0), block(0), pl.BlockSpec((8, width), lambda p: (0, p))],
        out_shape=[one, one, one, jax.ShapeDtypeStruct((8, pairs * width), f32)],
        scratch_shapes=[pltpu.VMEM((length, length), bf16)],
        compiler_params=pltpu.CompilerParams(vmem_limit_bytes=VMEM_LIMIT),
        name="attend_back",
    )(joined, joined, joined, et, inverse, grad_context, context)


def mean_of(values):
    return jnp.mean(values, axis=-1, keepdims=True)


def mlp_kernel(
    len_ref,
    ctx_ref,
    stem_ref,
    w_out_ref,
    b_out_ref,
    gain_ref,
    bias_ref,
    w_up_ref,
    b_up_ref,
    w_down_ref,
    b_down_ref,
    target_ref,
    out_ref,
    gctx_ref,
    gmid_ref,
    gw_up_ref,
    gw_down_ref,
    gw_out_ref,
    sums_ref,
    gb_up_ref,
    mid_ref,
    normed_ref,
    normed_t_ref,
    hidden_ref,
    slope_ref,
    branch_ref,
    branch_t_ref,
):
    length, width = ctx_ref.shape
    inner = w_up_ref.shape[1]
    row_steps, tile_steps = length // BLOCK, inner // BLOCK
    ones = lambda v: jnp.sum(v, axis=0, keepdims=True)
    sums_ref[...] = jnp.zeros_like(sums_ref)

    @pl.loop(0, row_steps)
    def _(i):
        rows = pl.ds(pl.multiple_of(i * BLOCK, BLOCK), BLOCK)
        middle = stem_ref[rows].astype(f32) + mm(ctx_ref[rows], w_out_ref[...]) + b_out_ref[...]
        mid_ref[rows] = middle
        centred = middle - mean_of(middle)
        scale = lax.rsqrt(mean_of(centred * centred) + epsilon)
        normed_ref[rows] = (centred * scale * gain_ref[...] + bias_ref[...]).astype(bf16)

    @pl.loop(0, tile_steps)
    def _(j):
        cols = pl.ds(pl.multiple_of(j * BLOCK, BLOCK), BLOCK)
        upward = mm(normed_ref[...], w_up_ref[:, cols]) + b_up_ref[:, cols]
        hidden, slope = gelu_pair(upward)
        hidden_ref[:, cols] = hidden.astype(bf16)
        slope_ref[:, cols] = slope.astype(bf16)

    @pl.loop(0, row_steps)
    def _(i):
        rows = pl.ds(pl.multiple_of(i * BLOCK, BLOCK), BLOCK)
        final = mid_ref[rows] + mm(hidden_ref[rows], w_down_ref[...]) + b_down_ref[...]
        out_ref[rows] = final.astype(bf16)
        frame = i * BLOCK + lax.broadcasted_iota(jnp.int32, final.shape, 0)
        mismatch = jnp.where(frame < len_ref[0], final - target_ref[rows].astype(f32), 0.0)
        gmid_ref[rows] = mismatch
        branch = mismatch.astype(bf16)
        branch_ref[rows] = branch
        branch_t_ref[:, rows] = turned(branch)
        normed_t_ref[:, rows] = turned(normed_ref[rows])
        sums_ref[0:1] += ones(mismatch * mismatch)
        sums_ref[1:2] += ones(branch.astype(f32))

    @pl.loop(0, tile_steps)
    def _(j):
        cols = pl.ds(pl.multiple_of(j * BLOCK, BLOCK), BLOCK)
        grad = mm_nt(branch_ref[...], w_down_ref[cols]) * slope_ref[:, cols].astype(f32)
        grad = grad.astype(bf16)
        gb_up_ref[:, cols] = ones(grad.astype(f32))
        gw_down_ref[:, cols] = mm(branch_t_ref[...], hidden_ref[:, cols]).astype(bf16)
        gw_up_ref[:, cols] = mm(normed_t_ref[...], grad).astype(bf16)
        slope_ref[:, cols] = grad

    @pl.loop(0, row_steps)
    def _(i):
        rows = pl.ds(pl.multiple_of(i * BLOCK, BLOCK), BLOCK)
        grad = mm_nt(slope_ref[rows], w_up_ref[...])
        middle = mid_ref[rows]
        centred = middle - mean_of(middle)
        scale = lax.rsqrt(mean_of(centred * centred) + epsilon)
        unit = centred * scale
        gained = grad * gain_ref[...]
        back = scale * (gained - mean_of(gained) - unit * mean_of(gained * unit))
        grad_middle = gmid_ref[rows] + back
        gmid_ref[rows] = grad_middle
        attended = grad_middle.astype(bf16)
        branch_ref[rows] = attended
        gctx_ref[rows] = mm_nt(attended, w_out_ref[...]).astype(bf16)
        normed_t_ref[:, rows] = turned(ctx_ref[rows])
        sums_ref[2:3] += ones(grad * unit)
        sums_ref[3:4] += ones(grad)
        sums_ref[4:5] += ones(attended.astype(f32))

    @pl.loop(0, width // BLOCK)
    def _(j):
        cols = pl.ds(pl.multiple_of(j * BLOCK, BLOCK), BLOCK)
        gw_out_ref[:, cols] = mm(normed_t_ref[...], branch_ref[:, cols]).astype(bf16)


def shifted(values, step, axis):
    length = values.shape[axis]
    moved = pltpu.roll(values, step % length, axis)
    place = lax.broadcasted_iota(jnp.int32, values.shape, axis)
    return jnp.where(place == (0 if step > 0 else length - 1), 0.0, moved)


def pick_frames(slots, frames, offset):
    slot = lax.broadcasted_iota(jnp.int32, (slots, frames), 0)
    frame = lax.broadcasted_iota(jnp.int32, (slots, frames), 1)
    return jnp.where(frame == 2 * slot + offset, 1.0, 0.0).astype(bf16)


def flat_taps(ref):
    return ref[...].reshape(-1, ref.shape[-1])


def stem_kernel(
    mel_ref,
    w_one_ref,
    b_one_ref,
    w_two_ref,
    b_two_ref,
    pos_ref,
    gain_ref,
    bias_ref,
    w_qkv_ref,
    b_query_ref,
    b_value_ref,
    taps_ref,
    act_even_ref,
    act_odd_ref,
    slope_even_ref,
    slope_odd_ref,
    slope_two_ref,
    stem_ref,
    normed_ref,
    joined_ref,
    behind_ref,
):
    length, width = stem_ref.shape
    steps = length // BLOCK
    mel = mel_ref[...].astype(f32)
    taps = jnp.concatenate([shifted(mel, 1, 1), mel, shifted(mel, -1, 1)], axis=0).astype(bf16)
    taps_ref[...] = taps
    w_one = flat_taps(w_one_ref)
    for offset, act_ref, slope_ref in (
        (0, act_even_ref, slope_even_ref),
        (1, act_odd_ref, slope_odd_ref),
    ):
        for i in range(steps):
            rows = slice(i * BLOCK, (i + 1) * BLOCK)
            frames = slice(2 * i * BLOCK, 2 * (i + 1) * BLOCK)
            picked = mm_nt(pick_frames(BLOCK, 2 * BLOCK, offset), taps[:, frames]).astype(bf16)
            act, slope = gelu_pair(mm(picked, w_one) + b_one_ref[...])
            act_ref[rows] = act.astype(bf16)
            slope_ref[rows] = slope.astype(bf16)
    for cols in chunks(width, BLOCK):
        behind_ref[:, cols] = shifted(act_odd_ref[:, cols].astype(f32), 1, 0).astype(bf16)

    @pl.loop(0, steps)
    def _(i):
        rows = pl.ds(pl.multiple_of(i * BLOCK, BLOCK), BLOCK)
        two = (
            mm(behind_ref[rows], w_two_ref[0])
            + mm(act_even_ref[rows], w_two_ref[1])
            + mm(act_odd_ref[rows], w_two_ref[2])
            + b_two_ref[...]
        )
        act, slope = gelu_pair(two)
        slope_two_ref[rows] = slope.astype(bf16)
        stem = (act + pos_ref[rows]).astype(bf16)
        stem_ref[rows] = stem
        stem = stem.astype(f32)
        centred = stem - mean_of(stem)
        scale = lax.rsqrt(mean_of(centred * centred) + epsilon)
        normed = (centred * scale * gain_ref[...] + bias_ref[...]).astype(bf16)
        normed_ref[rows] = normed
        query, key, value = (slice(part * width, (part + 1) * width) for part in range(3))
        joined_ref[rows, query] = (mm(normed, w_qkv_ref[:, query]) + b_query_ref[...]).astype(bf16)
        joined_ref[rows, key] = mm(normed, w_qkv_ref[:, key]).astype(bf16)
        joined_ref[rows, value] = (mm(normed, w_qkv_ref[:, value]) + b_value_ref[...]).astype(bf16)


def stem_back_kernel(
    gq_ref,
    gk_ref,
    gv_ref,
    w_qkv_ref,
    gmid_ref,
    stem_ref,
    normed_ref,
    gain_ref,
    slope_two_ref,
    w_two_ref,
    act_even_ref,
    act_odd_ref,
    slope_even_ref,
    slope_odd_ref,
    w_one_ref,
    taps_ref,
    gw_qkv_ref,
    gw_two_ref,
    gw_one_ref,
    gmel_ref,
    sums_ref,
    normed_t_ref,
    two_ref,
    two_ahead_ref,
    two_t_ref,
    two_ahead_t_ref,
    even_ref,
    odd_ref,
):
    length, width = stem_ref.shape
    steps = length // BLOCK
    ones = lambda v: jnp.sum(v, axis=0, keepdims=True)
    sums_ref[...] = jnp.zeros_like(sums_ref)

    @pl.loop(0, steps)
    def _(i):
        rows = pl.ds(pl.multiple_of(i * BLOCK, BLOCK), BLOCK)
        normed_t_ref[:, rows] = turned(normed_ref[rows])
        grad = (
            mm_nt(gq_ref[rows], w_qkv_ref[:, 0:width])
            + mm_nt(gk_ref[rows], w_qkv_ref[:, width : 2 * width])
            + mm_nt(gv_ref[rows], w_qkv_ref[:, 2 * width : 3 * width])
        )
        stem = stem_ref[rows].astype(f32)
        centred = stem - mean_of(stem)
        scale = lax.rsqrt(mean_of(centred * centred) + epsilon)
        unit = centred * scale
        gained = grad * gain_ref[...]
        back = scale * (gained - mean_of(gained) - unit * mean_of(gained * unit))
        grad_stem = (gmid_ref[rows] + back).astype(bf16).astype(f32)
        two = (grad_stem * slope_two_ref[rows].astype(f32)).astype(bf16)
        two_ref[rows] = two
        two_t_ref[:, rows] = turned(two)
        sums_ref[0:1] += ones(grad * unit)
        sums_ref[1:2] += ones(grad)
        sums_ref[2:3] += ones(two.astype(f32))

    for cols in chunks(width, BLOCK):
        two_ahead_ref[:, cols] = shifted(two_ref[:, cols].astype(f32), -1, 0).astype(bf16)

    @pl.loop(0, steps)
    def _(i):
        rows = pl.ds(pl.multiple_of(i * BLOCK, BLOCK), BLOCK)
        two_ahead_t_ref[:, rows] = turned(two_ahead_ref[rows])
        even = mm_nt(two_ref[rows], w_two_ref[1]) * slope_even_ref[rows].astype(f32)
        odd = mm_nt(two_ref[rows], w_two_ref[2]) + mm_nt(two_ahead_ref[rows], w_two_ref[0])
        odd = odd * slope_odd_ref[rows].astype(f32)
        even_ref[rows] = even.astype(bf16)
        odd_ref[rows] = odd.astype(bf16)
        sums_ref[3:4] += ones(even.astype(bf16).astype(f32)) + ones(odd.astype(bf16).astype(f32))

    @pl.loop(0, width // BLOCK)
    def _(j):
        cols = pl.ds(pl.multiple_of(j * BLOCK, BLOCK), BLOCK)
        for part, grad_ref in enumerate((gq_ref, gk_ref, gv_ref)):
            out = pl.ds(pl.multiple_of(part * width + j * BLOCK, BLOCK), BLOCK)
            gw_qkv_ref[:, out] = mm(normed_t_ref[...], grad_ref[:, cols]).astype(bf16)
        gw_two_ref[0, :, cols] = mm(two_ahead_t_ref[...], act_odd_ref[:, cols]).astype(bf16)
        gw_two_ref[1, :, cols] = mm(two_t_ref[...], act_even_ref[:, cols]).astype(bf16)
        gw_two_ref[2, :, cols] = mm(two_t_ref[...], act_odd_ref[:, cols]).astype(bf16)

    bins = w_one_ref.shape[1]
    gw_one = jnp.zeros((3 * bins, width), f32)
    for offset, grad_ref in ((0, even_ref), (1, odd_ref)):
        picked = [
            mm_nt(taps_ref[:, 2 * i * BLOCK : 2 * (i + 1) * BLOCK], pick_frames(BLOCK, 2 * BLOCK, offset))
            for i in range(steps)
        ]
        gw_one += mm(jnp.concatenate(picked, axis=1).astype(bf16), grad_ref[...])
    gw_one_ref[...] = gw_one.astype(bf16).reshape(gw_one_ref.shape)
    even, odd = even_ref[...], odd_ref[...]
    mel_even = (
        mm_nt(odd, w_one_ref[0])
        + mm_nt(even, w_one_ref[1])
        + shifted(mm_nt(odd, w_one_ref[2]), 1, 0)
    )
    mel_odd = (
        shifted(mm_nt(even, w_one_ref[0]), -1, 0)
        + mm_nt(odd, w_one_ref[1])
        + mm_nt(even, w_one_ref[2])
    )
    mel_even, mel_odd = turned(mel_even), turned(mel_odd)
    for i in range(steps):
        cols = slice(i * BLOCK, (i + 1) * BLOCK)
        frames = slice(2 * i * BLOCK, 2 * (i + 1) * BLOCK)
        gmel_ref[:, frames] = (
            mm(mel_even[:, cols], pick_frames(BLOCK, 2 * BLOCK, 0))
            + mm(mel_odd[:, cols], pick_frames(BLOCK, 2 * BLOCK, 1))
        ).astype(bf16)


def run_whole(kernel, name, operands, results, scratch):
    held = pl.BlockSpec(memory_space=pltpu.VMEM)
    scalar = pl.BlockSpec(memory_space=pltpu.SMEM)
    return pl.pallas_call(
        kernel,
        in_specs=[scalar if o.dtype == jnp.int32 else held for o in operands],
        out_specs=[held] * len(results),
        out_shape=[jax.ShapeDtypeStruct(*r) for r in results],
        scratch_shapes=[pltpu.VMEM(*s) for s in scratch],
        compiler_params=pltpu.CompilerParams(vmem_limit_bytes=VMEM_LIMIT),
        name=name,
    )(*operands)


def on_device(
    mel_input,
    w_conv1,
    b_conv1,
    w_conv2,
    b_conv2,
    gain_attn,
    bias_attn,
    w_qkv,
    b_query,
    b_value,
    w_out,
    b_out,
    gain_mlp,
    bias_mlp,
    w_up,
    b_up,
    w_down,
    b_down,
    target,
    lengths,
    row_clip,
    language,
):
    clip_count, frame_count, model_width = target.shape
    mel_count = mel_input.shape[2]
    row_at = lax.axis_index("dp") * lax.axis_size("chan") + lax.axis_index("chan")
    own_id = lax.dynamic_index_in_dim(row_clip, row_at * clip_count, keepdims=False)
    valid_len = lookup(own_id, lengths)
    own_lang = lookup(own_id, language)

    mel = lax.all_to_all(mel_input, "chan", split_axis=1, concat_axis=0, tiled=True)[:, 0]
    bins = w_conv1.shape[1]
    line = lambda v: v.astype(f32).reshape(1, -1)
    square = (frame_count, model_width)
    (
        taps,
        act_even,
        act_odd,
        slope_even,
        slope_odd,
        slope_two,
        stem,
        normed_a,
        joined,
    ) = run_whole(
        stem_kernel,
        "stem",
        (
            mel,
            w_conv1,
            line(b_conv1),
            w_conv2,
            line(b_conv2),
            sinusoids(frame_count, model_width),
            line(gain_attn),
            line(bias_attn),
            w_qkv,
            line(b_query),
            line(b_value),
        ),
        [((3 * bins, mel_count), bf16)] + [(square, bf16)] * 7 + [((frame_count, 3 * model_width), bf16)],
        [(square, bf16)],
    )
    valid = valid_len.reshape(1)
    context, weights_t, inverse = attend(joined, valid)
    inner = w_up.shape[1]
    deep = (model_width, inner)
    (
        block_rows,
        grad_context,
        grad_middle,
        grad_w_up,
        grad_w_down_t,
        grad_w_out,
        sums_b,
        grad_b_up,
    ) = run_whole(
        mlp_kernel,
        "mlp",
        (
            valid,
            context,
            stem,
            w_out,
            line(b_out),
            line(gain_mlp),
            line(bias_mlp),
            w_up,
            line(b_up),
            w_down,
            line(b_down),
            target[0],
        ),
        [
            (square, bf16),
            (square, bf16),
            (square, f32),
            (deep, bf16),
            (deep, bf16),
            ((model_width, model_width), bf16),
            ((8, model_width), f32),
            ((1, inner), f32),
        ],
        [
            (square, f32),
            (square, bf16),
            (square, bf16),
            ((frame_count, inner), bf16),
            ((frame_count, inner), bf16),
            (square, bf16),
            (square, bf16),
        ],
    )
    clip_loss = 0.5 * jnp.sum(sums_b[0])
    grad_b_down, grad_gain_mlp, grad_bias_mlp, grad_b_out = (sums_b[i] for i in range(1, 5))
    grad_b_up = grad_b_up[0]
    group_ids = jnp.arange(GROUPS, dtype=jnp.int32)
    group_part = jnp.where(own_lang == group_ids, clip_loss, 0.0)

    *grads, sums_a = attend_back(joined, weights_t, inverse, grad_context, context)
    grad_b_query, grad_b_value = sums_a[0], sums_a[1]
    weight = (model_width, model_width)
    grad_w_qkv, grad_w_two_t, grad_w_one, back_mel, sums_c = run_whole(
        stem_back_kernel,
        "stem_back",
        (
            *grads,
            w_qkv,
            grad_middle,
            stem,
            normed_a,
            line(gain_attn),
            slope_two,
            w_conv2,
            act_even,
            act_odd,
            slope_even,
            slope_odd,
            w_conv1,
            taps,
        ),
        [
            ((model_width, 3 * model_width), bf16),
            ((3,) + weight, bf16),
            (w_conv1.shape, bf16),
            ((bins, mel_count), bf16),
            ((8, model_width), f32),
        ],
        [
            ((model_width, frame_count), bf16),
            (square, bf16),
            (square, bf16),
            ((model_width, frame_count), bf16),
            ((model_width, frame_count), bf16),
            (square, bf16),
            (square, bf16),
        ],
    )
    grad_gain_attn, grad_bias_attn, grad_b_two, grad_b_one = (sums_c[i] for i in range(4))
    grad_mel = lax.all_to_all(back_mel[:, None], "chan", split_axis=0, concat_axis=1, tiled=True)

    def scatter(values, dp_at, chan_at):
        part = lax.psum_scatter(values, "dp", scatter_dimension=dp_at, tiled=True)
        return lax.psum_scatter(part, "chan", scatter_dimension=chan_at, tiled=True).astype(f32)

    final_down = scatter(grad_w_down_t, 1, 0).T
    final_up = scatter(grad_w_up, 0, 1)
    final_out = scatter(grad_w_out, 0, 1)
    final_qkv = scatter(grad_w_qkv, 0, 1)
    part_two = scatter(grad_w_two_t, 1, 2).transpose(0, 2, 1)
    part_one = scatter(grad_w_one, 2, 1)
    totals_all = lax.psum(
        (
            group_part,
            grad_b_one,
            grad_b_two,
            grad_gain_attn,
            grad_bias_attn,
            grad_b_query,
            grad_b_value,
            grad_b_out,
            grad_gain_mlp,
            grad_bias_mlp,
            grad_b_up,
            grad_b_down,
        ),
        ("dp", "chan"),
    )
    member_all = language[:, None] == group_ids[None, :]
    frames_group = jnp.sum(jnp.where(member_all, lengths[:, None], 0), axis=0)
    group_loss = totals_all[0] / (model_width * jnp.maximum(frames_group, 1).astype(f32))
    return (
        block_rows.reshape(target.shape),
        group_loss,
        grad_mel,
        part_one,
        totals_all[1],
        part_two,
        totals_all[2],
        totals_all[3],
        totals_all[4],
        final_qkv,
        totals_all[5],
        totals_all[6],
        final_out,
        totals_all[7],
        totals_all[8],
        totals_all[9],
        final_up,
        totals_all[10],
        final_down,
        totals_all[11],
    )


def solution(mesh):
    whole = P()
    by_row = P(("dp", "chan"), None, None)
    return jax.shard_map(
        on_device,
        mesh=mesh,
        in_specs=(P("chan", "dp", None),) + (whole,) * 17 + (by_row,) + (whole,) * 3,
        out_specs=(
            by_row,
            whole,
            P("chan", "dp", None),
            P(None, "chan", "dp"),
            whole,
            P(None, "chan", "dp"),
            whole,
            whole,
            whole,
            P("dp", "chan"),
            whole,
            whole,
            P("dp", "chan"),
            whole,
            whole,
            whole,
            P("dp", "chan"),
            whole,
            P("dp", "chan"),
            whole,
        ),
        check_vma=False,
    )
```

time: 757 us -> 565 us (0.75)
  matrix products: 306 us -> 0 us
  Pallas kernels: 0 us -> 154 us
  waiting for transfers between devices: 163 us -> 265 us
  other arithmetic: 97.7 us -> 11.3 us
  local copies, waits for them, and re-layouts: 91.2 us -> 39.7 us
    dot_general x113 -> x0, matrix products: 306 us -> none  [the longest x37 119 us: mm(): return jnp.dot(a, b, preferred_element_type=f32)]
    pallas_call x0 -> x5, Pallas kernels: none -> 154 us  [the longest x3 110 us: run_whole(): pl.pallas_call(kernel, in_specs=[scalar if o.dtype == jnp.int32 else held...]
    reduce_scatter x4, waiting for transfers between devices: 99.4 us -> 142 us  [scatter(): part = lax.psum_scatter(values, 'dp', scatter_dimension=dp_at, tiled=True)]
    unnamed x16, waiting for transfers between devices: 44.2 us -> 81 us
    convert_element_type x23 -> x0, other arithmetic: 32.3 us -> none  [the longest x12 20.1 us: attend_back(): grad_scores = (weight * (grad_attention - inner)).astype(bf16)]
    unnamed x160 -> x48, local copies, waits for them, and re-layouts: 52 us -> 27.1 us
    reduce_scatter x2, waiting for transfers between devices: 19.2 us -> 41.7 us  [scatter(): lax.psum_scatter(part, 'chan', scatter_dimension=chan_at, tiled=True)]
    reduce_sum x20 -> x0, other arithmetic: 22.2 us -> none  [the longest x4 12.2 us: column_sum(): return jnp.sum(values.astype(f32), axis=0)]
  transfers between devices with their start and end apart: 13 -> 13, of which waited for: 5 -> 8; matrix products, arithmetic and copies ran while one was open for 38% -> 8% of each run, Pallas kernels for 0% -> 8%
where the time goes in v2:
time: 565 us; the launch traced here: 558 us
  waiting for transfers between devices  265 us (47%)
  Pallas kernels  154 us (27%)
  blocking collectives  60.8 us (11%)
  local copies, waits for them, and re-layouts  39.7 us (7%)
  between operations  15.9 us (3%)
  starting transfers between devices  11.6 us (2%)
  other arithmetic  11.3 us (2%)
    reduce_scatter x4, waiting for transfers between devices, scatter(): part = lax.psum_scatter(values, 'dp', scatter_dimension=dp_at, tiled=True)  142 us
    pallas_call x3, Pallas kernels, run_whole(): pl.pallas_call(kernel, in_specs=[scalar if o.dtype == jnp.int32 else held...  110 us
    unnamed x16, waiting for transfers between devices  81 us
    reduce_scatter x2, waiting for transfers between devices, scatter(): lax.psum_scatter(part, 'chan', scatter_dimension=chan_at, tiled=True)  41.7 us
    psum x1, blocking collectives, on_device(): lax.psum((group_part, grad_b_one, grad_b_two, grad_gain_attn, grad_bias_a...  41.5 us
    unnamed x48, local copies, waits for them, and re-layouts  27.1 us
    pallas_call x1, Pallas kernels, attend(): pl.pallas_call(attend_kernel, grid_spec=pltpu.PrefetchScalarGridSpec(num_...  25.3 us
    unnamed x1, blocking collectives  19.3 us
  transfers between devices with their start and end apart: 13, of which 8 were waited for; matrix products, arithmetic and copies ran while one was open for 8% of the time, Pallas kernels for 8%

profile of v2, /device:TPU:0, one launch (start us, length us, event | category | flops | bytes accessed | tf_op | source)
XLA Modules:
  0.0 558.1 jit_solution(7618007804827074559)
XLA Ops:
  7.3 1.7 copy.53
  9.0 6.3 %all-to-all-start = ((bf16[20,4,1536]{2,0,1:T(8,128)(2,1)}), bf16[20,4,1536]{2,0,1:T(8,128)(2,1)S(1)}, u32[]{:S(2)}, u32[]{:S(2)}) async-start(bf16[20,4,1536]{2,0,1:T(8,128)(2,1)} %copy.53), calls=%async_computation | async-start | bytes 589824 | tf_op jit(solution)/shard_map/all_to_all | solution.py:550
  28.5 24.1 %stem.1 = (bf16[240,1536]{1,0:T(8,128)(2,1)}, bf16[768,768]{1,0:T(8,128)(2,1)}, bf16[768,768]{1,0:T(8,128)(2,1)}, bf16[768,768]{1,0:T(8,128)(2,1)}, bf16[768,768...) custom-call(bf16[80,1536]{1,0:T(8,128)(2,1)} %squeeze.45.mel_ref, ...), custom_call_target="tpu_custom_call" | custom-call | tf_op jit(solution)/shard_map/stem/pallas_call | solution.py:508
  52.6 25.3 %attend.1 = (bf16[768,768]{1,0:T(8,128)(2,1)}, bf16[12,768,768]{2,1,0:T(8,128)(2,1)}, f32[12,1,768]{2,1,0:T(1,128)}) custom-call(s32[1]{0:T(128)} %bitcast.13.len_ref, bf16[768,2304]{1,0:T(8,128)(2,1)} %get-tuple-element.49.q_ref.k_ref.v_ref, bf16[768,2304]{1,0:T(8,128)(2,1)} %get-tuple-element.49.q_ref.k_ref.v_ref, ...), custom_call_target="tpu_custom_call" | custom-call | tf_op jit(solution)/shard_map/attend/pallas_call | solution.py:155
  77.9 59.2 %mlp.1 = (bf16[768,768]{1,0:T(8,128)(2,1)}, bf16[768,768]{1,0:T(8,128)(2,1)}, f32[768,768]{1,0:T(8,128)}, bf16[768,3072]{1,0:T(8,128)(2,1)}, bf16[768,3072]{1,0:...) custom-call(s32[1]{0:T(128)} %bitcast.13.len_ref, ...), custom_call_target="tpu_custom_call" | custom-call | tf_op jit(solution)/shard_map/mlp/pallas_call | solution.py:508
  137.1 18.6 %attend_back.1 = (bf16[768,768]{1,0:T(8,128)(2,1)}, bf16[768,768]{1,0:T(8,128)(2,1)}, bf16[768,768]{1,0:T(8,128)(2,1)}, f32[8,768]{1,0:T(8,128)}) custom-call(bf16[768,2304]{1,0:T(8,128)(2,1)} %get-tuple-element.49.q_ref.k_ref.v_ref, bf16[768,2304]{1,0:T(8,128)(2,1)} %get-tuple-element.49.q_ref.k_ref.v_ref, ...), custom_call_target="tpu_custom_call" | custom-call | tf_op jit(solution)/shard_map/attend_back/pallas_call | solution.py:182
  155.7 27.1 %stem_back.1 = (bf16[768,2304]{1,0:T(8,128)(2,1)}, bf16[3,768,768]{2,1,0:T(8,128)(2,1)}, bf16[3,80,768]{2,1,0:T(8,128)(2,1)}, bf16[80,1536]{1,0:T(8,128)(2,1)}, f32[8,768]{1,0:T(8,128)}) custom-call(bf16[768,768]{1,0:T(8,128)(2,1)} %get-tuple-element.57.gq_ref, bf16[768,768]{1,0:T(8,128)(2,1)} %get-tuple-element.58.gk_ref, ...), custom_call_target="tpu_custom_call" | custom-call | tf_op jit(solution)/shard_map/stem_back/pallas_call | solution.py:508
  184.2 6.6 %copy.67 = bf16[768,3072]{0,1:T(8,128)(2,1)} copy(bf16[768,3072]{1,0:T(8,128)(2,1)} %get-tuple-element.77) | data formatting | bytes 9437184
  193.6 1.7 copy.65
  195.4 37.2 %reduce-scatter.23.cloned.1.call-done = bf16[3,96,768]{2,1,0:T(8,128)(2,1)} async-done(((bf16[3,768,768]{2,1,0:T(8,128)(2,1)}), bf16[3,96,768]{2,1,0:T(8,128)(2,1)}) %reduce-scatter.23.cloned.1.call-update) | async-done | bytes 442384 | tf_op jit(solution)/shard_map/reduce_scatter | solution.py:682
  235.4 49.2 %reduce-scatter.25.cloned.1.call-done = bf16[96,2304]{1,0:T(8,128)(2,1)} async-done(((bf16[768,2304]{1,0:T(8,128)(2,1)}), bf16[96,2304]{1,0:T(8,128)(2,1)}) %reduce-scatter.25.cloned.1.call-update) | async-done | bytes 442384 | tf_op jit(solution)/shard_map/reduce_scatter | solution.py:682
  284.6 2.1 copy.63
  286.7 55.5 %reduce-scatter.29.cloned.1.call-done = bf16[96,3072]{1,0:T(8,128)(2,1)} async-done(((bf16[768,3072]{1,0:T(8,128)(2,1)}), bf16[96,3072]{1,0:T(8,128)(2,1)}) %reduce-scatter.29.cloned.1.call-update) | async-done | bytes 589840 | tf_op jit(solution)/shard_map/reduce_scatter | solution.py:682
  343.8 55.6 %reduce-scatter.43.cloned.1.call-done = bf16[384,768]{1,0:T(8,128)(2,1)} async-done(((bf16[3072,768]{1,0:T(8,128)(2,1)}), bf16[384,768]{1,0:T(8,128)(2,1)}) %reduce-scatter.43.cloned.1.call-update) | async-done | bytes 589840
  399.4 2.1 copy.68
  403.7 4.6 all-to-all-start.1
  411.2 41.5 %all-reduce.1 = (f32[99]{0:T(128)S(1)}, f32[768]{0:T(1024)}, f32[768]{0:T(1024)}, f32[768]{0:T(1024)}, f32[768]{0:T(1024)}, /*index=5*/f32[768]{0:T(1024)}, f32[...) all-reduce(f32[99]{0:T(128)S(1)} %compare_select_fusion, ...), channel_id=1, replica_groups=mesh['dp'=8,'chan'=4] {'dp','chan'}, use_global_device_ids=true, to_apply=%region_3.4 | all-reduce | flops 10851 | bytes 86808 | tf_op jit(solution)/shard_map/psum | solution.py:691
  456.8 19.3 %all-reduce = bf16[3,80,96]{2,1,0:T(8,128)(2,1)S(1)} all-reduce(bf16[3,80,96]{2,1,0:T(8,128)(2,1)S(1)} %copy.58), channel_id=3, replica_groups=mesh['dp'=8,'chan'=4] {'chan'}, use_global_device_ids=true, to_apply=%region_6.7.clone | all-reduce | flops 23040 | bytes 92160
  478.3 3.5 reduce-scatter.37.cloned.1.call-done
  483.8 20.6 %reduce-scatter.39.cloned.1.call-done = bf16[576,96]{1,0:T(8,128)(2,1)} async-done(((bf16[2304,96]{1,0:T(8,128)(2,1)}), bf16[576,96]{1,0:T(8,128)(2,1)}) %reduce-scatter.39.cloned.1.call-update) | async-done | bytes 110608
  506.2 20.7 %reduce-scatter.31.cloned.1.call-done = bf16[96,768]{1,0:T(8,128)(2,1)} async-done(((bf16[96,3072]{1,0:T(8,128)(2,1)}), bf16[96,768]{1,0:T(8,128)(2,1)}) %reduce-scatter.31.cloned.1.call-update) | async-done | bytes 147472 | tf_op jit(solution)/shard_map/reduce_scatter | solution.py:683
  526.9 1.6 convert_element_type.14
  528.5 21.0 %reduce-scatter.33.cloned.1.call-done = bf16[192,384]{1,0:T(8,128)(2,1)} async-done(((bf16[768,384]{1,0:T(8,128)(2,1)}), bf16[192,384]{1,0:T(8,128)(2,1)}) %reduce-scatter.33.cloned.1.call-update) | async-done | bytes 147472 | tf_op jit(solution)/shard_map/reduce_scatter | solution.py:683
  549.5 1.6 convert_bitcast_fusion
  (98 shorter events, 35.5 us)
Async XLA Ops:
  7.2 15.7 %copy-start.6 = (bf16[768]{0:T(1024)(128)(2,1)S(1)}, bf16[768]{0:T(1024)(128)(2,1)}, u32[]{:S(2)}) copy-start(bf16[768]{0:T(1024)(128)(2,1)} %param.34) | copy-start | bytes 4612
  7.2 16.3 %copy-start.7 = (bf16[768]{0:T(1024)(128)(2,1)S(1)}, bf16[768]{0:T(1024)(128)(2,1)}, u32[]{:S(2)}) copy-start(bf16[768]{0:T(1024)(128)(2,1)} %param.35) | copy-start | bytes 4612
  7.2 16.9 %copy-start.8 = (bf16[768]{0:T(1024)(128)(2,1)S(1)}, bf16[768]{0:T(1024)(128)(2,1)}, u32[]{:S(2)}) copy-start(bf16[768]{0:T(1024)(128)(2,1)} %param.36) | copy-start | bytes 4612
  7.2 17.4 %copy-start.5 = (bf16[3072]{0:T(1024)(128)(2,1)S(1)}, bf16[3072]{0:T(1024)(128)(2,1)}, u32[]{:S(2)}) copy-start(bf16[3072]{0:T(1024)(128)(2,1)} %param.38) | copy-start | bytes 18436
  7.2 18.0 %copy-start.9 = (bf16[768]{0:T(1024)(128)(2,1)S(1)}, bf16[768]{0:T(1024)(128)(2,1)}, u32[]{:S(2)}) copy-start(bf16[768]{0:T(1024)(128)(2,1)} %param.40) | copy-start | bytes 4612
  7.2 18.6 %copy-start.12 = (s32[32]{0:T(128)S(1)}, s32[32]{0:T(128)}, u32[]{:S(2)}) copy-start(s32[32]{0:T(128)} %param.43) | copy-start | bytes 388
  7.3 19.2 %copy-start.10 = (s32[32]{0:T(128)S(1)}, s32[32]{0:T(128)}, u32[]{:S(2)}) copy-start(s32[32]{0:T(128)} %param.42) | copy-start | bytes 388
  7.3 19.2 %copy-start.11 = (s32[32]{0:T(128)S(1)}, s32[32]{0:T(128)}, u32[]{:S(2)}) copy-start(s32[32]{0:T(128)} %param.44) | copy-start | bytes 388
  9.0 18.7 %all-to-all-start = ((bf16[20,4,1536]{2,0,1:T(8,128)(2,1)}), bf16[20,4,1536]{2,0,1:T(8,128)(2,1)S(1)}, u32[]{:S(2)}, u32[]{:S(2)}) async-start(bf16[20,4,1536]{2,0,1:T(8,128)(2,1)} %copy.53), calls=%async_computation | async-start | bytes 589824 | tf_op jit(solution)/shard_map/all_to_all | solution.py:550
  15.3 178.3 %reduce-scatter.27.cloned.1.call-start = ((), (), s32[]{:S(2)}) async-start(), calls=%async_computation.15 | async-start | bytes 1327104 | tf_op jit(solution)/shard_map/reduce_scatter | solution.py:682
  137.1 95.5 %reduce-scatter.23.cloned.1.call-start = ((), (), s32[]{:S(2)}) async-start(), calls=%async_computation.13 | async-start | bytes 3981312 | tf_op jit(solution)/shard_map/reduce_scatter | solution.py:682
  182.8 101.8 %reduce-scatter.25.cloned.1.call-start = ((), (), s32[]{:S(2)}) async-start(), calls=%async_computation.14 | async-start | bytes 3981312 | tf_op jit(solution)/shard_map/reduce_scatter | solution.py:682
  183.5 158.6 %reduce-scatter.29.cloned.1.call-start = ((), (), s32[]{:S(2)}) async-start(), calls=%async_computation.16 | async-start | bytes 5308416 | tf_op jit(solution)/shard_map/reduce_scatter | solution.py:682
  184.1 215.3 %reduce-scatter.43.cloned.1.call-start = ((), (), s32[]{:S(2)}) async-start(), calls=%async_computation.23 | async-start | bytes 5308416
  190.8 265.0 %reduce-scatter.35.cloned.1.call-start = ((), (), s32[]{:S(2)}) async-start(), calls=%async_computation.19 | async-start | bytes 442368
  193.5 283.2 %reduce-scatter.41.cloned.1.call-start = ((), (), s32[]{:S(2)}) async-start(), calls=%async_computation.22 | async-start | bytes 245760
  195.4 286.4 %reduce-scatter.37.cloned.1.call-start = ((), (), s32[]{:S(2)}) async-start(), calls=%async_computation.20 | async-start | bytes 737280
  235.3 107.2 %copy-start.13 = (u32[32]{0:T(128)S(1)}, u32[32]{0:T(128)}, u32[]{:S(2)}) copy-start(u32[32]{0:T(128)} %constant.33) | copy-start | bytes 388
  235.3 269.1 %reduce-scatter.39.cloned.1.call-start = ((), (), s32[]{:S(2)}) async-start(), calls=%async_computation.21 | async-start | bytes 737280
  286.7 240.2 %reduce-scatter.31.cloned.1.call-start = ((), (), s32[]{:S(2)}) async-start(), calls=%async_computation.17 | async-start | bytes 737280 | tf_op jit(solution)/shard_map/reduce_scatter | solution.py:683
  342.2 60.0 %copy-start.1 = (bf16[80,1536]{1,0:T(8,128)(2,1)S(1)}, bf16[80,1536]{1,0:T(8,128)(2,1)}, u32[]{:S(2)}) copy-start(bf16[80,1536]{1,0:T(8,128)(2,1)} %get-tuple-element.68) | copy-start | bytes 737284
  342.2 207.3 %reduce-scatter.33.cloned.1.call-start = ((), (), s32[]{:S(2)}) async-start(), calls=%async_computation.18 | async-start | bytes 737280 | tf_op jit(solution)/shard_map/reduce_scatter | solution.py:683
  401.5 9.6 %copy-start.2 = (f32[1,3072]{1,0:T(1,128)S(1)}, f32[1,3072]{1,0:T(1,128)}, u32[]{:S(2)}) copy-start(f32[1,3072]{1,0:T(1,128)} %get-tuple-element.76) | copy-start | bytes 36868
  403.7 49.5 %all-to-all-start.1 = ((bf16[4,2,15360]{2,1,0:T(2,128)(2,1)}), bf16[4,2,15360]{2,1,0:T(2,128)(2,1)S(1)}, u32[]{:S(2)}, u32[]{:S(2)}) async-start(bf16[4,2,15360]{2,1,0:T(2,128)(2,1)} %reshape.175), calls=%async_computation.1 | async-start | bytes 491520 | tf_op jit(solution)/shard_map/all_to_all | solution.py:679
  (3 other events, 17.4 us)
Sparse Core Ops, SparseCore 0:
  137.2 38.2 reduce-scatter.26
  182.9 49.5 reduce-scatter.22
  236.5 48.0 reduce-scatter.24
  288.3 53.8 reduce-scatter.28
  345.5 53.8 reduce-scatter.42
  402.6 33.8 reduce-scatter.34
  439.4 19.3 reduce-scatter.40
  461.1 20.6 reduce-scatter.36
  484.0 20.3 reduce-scatter.38
  506.5 20.2 reduce-scatter.30
  529.2 20.2 reduce-scatter.32
